TPU v7x, 512 devices: a whole 4x4x16 slice. The times are simulated.
512 devices in a mesh: img: 64 (over z, x), aug: 8 (over y, core).
Axes of the slice: x: 4, y: 4, z: 16, core: 2. Of those that a mesh axis runs over, the one named last changes fastest.
Arguments:
- activations: bfloat16 [64, 8, 197, 768], P('img', 'aug'), may hold values from -8 to 8
- out_grads: bfloat16 [64, 8, 197, 3072], P('img', 'aug'), may hold values from -0.33 to 0.33
- kept_mask: int32 [64, 8], P('img', 'aug'), may hold values from 0 to 1, as said below
- noise_field: float32 [768, 3072], P('img', 'aug'), may hold values from -6 to 6
Outputs:
- clipped_sum: float32 [768, 3072], P('img', 'aug')
- update: float32 [768, 3072], P('img', 'aug')
- norms: float32 [64], P('img')
Inputs may be any that keep to these rules, and one draw needn't show every extreme that they name: `kept_mask`: every image keeps at least one of its 8 copies.
All inputs are finite; a program needn't handle non-finite values.
Results may differ from a plain program's by a relative error of at most 0.00035.
Values may be sent and summed in bfloat16 or wider, within the bound.
A program may use at most 64 MiB of HBM per device.

v0:
```python
import math

import jax
import jax.numpy as jnp
from jax import lax
from jax.sharding import PartitionSpec as P


def per_device(activations, out_grads, kept_mask, noise_field):
    aug_count = lax.axis_size("aug")
    image_count = lax.axis_size("img")
    own_acts = activations[0, 0]
    own_grads = out_grads[0, 0]
    own_weight = kept_mask[0, 0].astype(jnp.float32)
    feature_count = activations.shape[3]
    hidden_count = out_grads.shape[3]
    block_width = hidden_count // aug_count
    clip_bound = 0.01 * math.sqrt(feature_count * hidden_count * activations.shape[2])
    aug_index = lax.axis_index("aug")
    act_piece = lax.all_gather(activations, "aug", axis=1, tiled=True)
    grad_piece = lax.all_gather(out_grads, "aug", axis=1, tiled=True)
    weight_piece = lax.all_gather(kept_mask, "aug", axis=1, tiled=True)
    weights = weight_piece[0]
    masked = act_piece[0] * weights.astype(jnp.bfloat16)[:, None, None]
    grad_block = lax.dynamic_slice_in_dim(grad_piece[0], aug_index * block_width, block_width, 2)
    grad_sum = jnp.einsum("nsd,nsf->df", masked, grad_block, preferred_element_type=jnp.float32)
    left_gram = jnp.einsum("sd,ntd->nst", own_acts, masked, preferred_element_type=jnp.float32)
    right_gram = jnp.einsum(
        "sf,ntf->nst", own_grads, grad_piece[0], preferred_element_type=jnp.float32
    )
    gram_part = jnp.sum(left_gram * right_gram)
    kept_count = jnp.sum(weights.astype(jnp.float32))
    grad_sum, gram_part, kept_count = (grad_sum, gram_part, kept_count)
    square = lax.psum(gram_part * own_weight, "aug")
    norm_value = jnp.sqrt(square) / kept_count
    mean_grad = grad_sum / kept_count
    factor = clip_bound / jnp.maximum(norm_value, clip_bound)
    clipped = lax.psum_scatter(factor * mean_grad, "img", scatter_dimension=0, tiled=True)
    update = (clipped + clip_bound * noise_field) / image_count
    return (clipped, update, norm_value.reshape(1))


def solution(mesh):
    in_specs = (
        P("img", "aug", None, None),
        P("img", "aug", None, None),
        P("img", "aug"),
        P("img", "aug"),
    )
    out_specs = (P("img", "aug"), P("img", "aug"), P("img"))
    return jax.shard_map(
        per_device, mesh=mesh, in_specs=in_specs, out_specs=out_specs, check_vma=False
    )
```

profile of v0, /device:TPU:70, one launch (start us, length us, event | category | flops | bytes accessed | tf_op | source)
XLA Modules:
  0.0 355.9 jit_solution(17842945964295289230)
XLA Ops:
  11.2 9.5 %all-reduce = s32[8]{0:T(128)S(1)} all-reduce(s32[8]{0:T(128)S(1)} %bitcast_dynamic-update-slice_fusion), channel_id=1, replica_groups=mesh['img'=64,'aug'=8] {'aug'}, use_global_device_ids=true, to_apply=%add | all-reduce | flops 8 | bytes 64
  21.4 55.9 %all-gather.5.cloned.1.call-done = bf16[1,8,197,3072]{3,2,0,1:T(8,128)(2,1)} async-done(((bf16[1,1,197,3072]{3,2,0,1:T(8,128)(2,1)}), bf16[1,8,197,3072]{3,2,0,1:T(8,128)(2,1)}) %all-gather.5.cloned.1.call-update) | async-done | bytes 9682960 | tf_op jit(solution)/shard_map/all_gather | solution.py:21
  77.3 5.8 %fusion.1 = f32[8,197,197]{2,1,0:T(8,128)S(1)} fusion(bf16[1,8,197,3072]{3,2,0,1:T(8,128)(2,1)} %all-gather.5.cloned.1.call-done, bf16[1,1,197,3072]{3,2,1,0:T(8,128)(2,1)} %param.5), kind=kOutput, calls=%fused_computation | convolution fusion | flops 1907539968 | bytes 12135200 | tf_op jit(solution)/shard_map/sf,ntf->nst/dot_general | solution.py:28
  83.1 30.2 %all-gather.3.cloned.1.call-done = bf16[1,8,197,768]{3,2,0,1:T(8,128)(2,1)} async-done(((bf16[1,1,197,768]{3,2,0,1:T(8,128)(2,1)}), bf16[1,8,197,768]{3,2,0,1:T(8,128)(2,1)}) %all-gather.3.cloned.1.call-update) | async-done | bytes 2420752 | tf_op jit(solution)/shard_map/all_gather | solution.py:20
  113.3 3.2 multiply_reduce_fusion
  117.1 14.5 %psum.7 = f32[]{:T(128)} all-reduce(f32[]{:T(128)S(6)} %mul.38), channel_id=1, replica_groups=mesh['img'=64,'aug'=8] {'aug'}, use_global_device_ids=true, to_apply=%region_1.0 | all-reduce | flops 1 | bytes 8 | tf_op jit(solution)/shard_map/psum | solution.py:34
  133.0 4.3 %divide_multiply_fusion = f32[768,384]{1,0:T(8,128)S(1)} fusion(bf16[1,8,197,3072]{3,2,0,1:T(8,128)(2,1)} %all-gather.5.cloned.1.call-done, s32[]{:T(128)S(6)} %select_n.3, bf16[1,8,197,768]{3,2,0,1:T(8,128)(2,1)} %all-gather.3.cloned.1.call-done, bf16[8]{0:T(256)(128)(2,1)S(1)} %convert_element_type.25, f32[]{:T(128)} %convert_reduce_fusion, f32[]{:T(128)S(6)} %div.19), kind=kOutput, calls=%fused_computation.15 | convolution fusion | flops 931362816 | bytes 4866584 | tf_op jit(solution)/shard_map/nsd,nsf->df/dot_general | solution.py:26
  137.4 142.5 %fusion = f32[16,384]{1,0:T(8,128)S(1)} fusion(f32[768,384]{1,0:T(8,128)S(1)} %divide_multiply_fusion), kind=kCustom, calls=%all-reduce-scatter | all-reduce-scatter fusion | flops 393217 | bytes 1206272
  279.9 8.4 %collective-permute-start.15 = (f32[12,384]{1,0:T(8,128)S(1)}, f32[12,384]{1,0:T(8,128)S(1)}, u32[]{:S(2)}, u32[]{:S(2)}) collective-permute-start(f32[12,384]{1,0:T(8,128)S(1)} %slice), channel_id=1, source_target_pairs={{0,128},{8,136},{16,144},{24,152},{32,160},{40,168},{48,176},{56,1... | collective-permute-start | bytes 55304
  288.3 6.0 %collective-permute-start = (f32[16,384]{1,0:T(8,128)S(1)}, f32[16,384]{1,0:T(8,128)S(1)}, u32[]{:S(2)}, u32[]{:S(2)}) collective-permute-start(f32[16,384]{1,0:T(8,128)S(1)} %fusion), channel_id=1, source_target_pairs={{0,8},{8,16},{16,24},{24,32},{32,40},{40,48},{48,56},{56,64},{64,7... | collective-permute-start | bytes 73736
  294.3 5.8 %collective-permute-start.1 = (f32[16,384]{1,0:T(8,128)S(1)}, f32[16,384]{1,0:T(8,128)S(1)}, u32[]{:S(2)}, u32[]{:S(2)}) collective-permute-start(f32[16,384]{1,0:T(8,128)S(1)} %fusion), channel_id=1, source_target_pairs={{0,16},{8,24},{16,32},{24,40},{32,48},{40,56},{48,64},{56,72},{64,... | collective-permute-start | bytes 73736
  300.0 1.9 collective-permute-start.10
  302.0 3.1 collective-permute-start.11
  305.1 7.9 %collective-permute-start.12 = (f32[16,384]{1,0:T(8,128)S(1)}, f32[16,384]{1,0:T(8,128)S(1)}, u32[]{:S(2)}, u32[]{:S(2)}) collective-permute-start(f32[16,384]{1,0:T(8,128)S(1)} %fusion), channel_id=1, source_target_pairs={{0,104},{8,112},{16,120},{24,128},{32,136},{40,144},{48,152},{56,1... | collective-permute-start | bytes 73736
  315.6 4.0 %collective-permute-start.2 = (f32[16,384]{1,0:T(8,128)S(1)}, f32[16,384]{1,0:T(8,128)S(1)}, u32[]{:S(2)}, u32[]{:S(2)}) collective-permute-start(f32[16,384]{1,0:T(8,128)S(1)} %fusion), channel_id=1, source_target_pairs={{0,24},{8,32},{16,40},{24,48},{32,56},{40,64},{48,72},{56,80},{64,... | collective-permute-start | bytes 73736
  319.6 2.7 collective-permute-start.3
  322.4 3.7 %collective-permute-start.4 = (f32[16,384]{1,0:T(8,128)S(1)}, f32[16,384]{1,0:T(8,128)S(1)}, u32[]{:S(2)}, u32[]{:S(2)}) collective-permute-start(f32[16,384]{1,0:T(8,128)S(1)} %fusion), channel_id=1, source_target_pairs={{0,40},{8,48},{16,56},{24,64},{32,72},{40,80},{48,88},{56,96},{64,... | collective-permute-start | bytes 73736
  326.2 2.4 collective-permute-start.5
  328.6 2.3 collective-permute-start.6
  330.9 1.9 collective-permute-start.7
  332.8 3.6 %collective-permute-start.8 = (f32[16,384]{1,0:T(8,128)S(1)}, f32[16,384]{1,0:T(8,128)S(1)}, u32[]{:S(2)}, u32[]{:S(2)}) collective-permute-start(f32[16,384]{1,0:T(8,128)S(1)} %fusion), channel_id=1, source_target_pairs={{0,72},{8,80},{16,88},{24,96},{32,104},{40,112},{48,120},{56,128},... | collective-permute-start | bytes 73736
  336.4 1.9 collective-permute-start.9
  340.3 5.1 %collective-permute-done.9 = f32[16,384]{1,0:T(8,128)S(1)} collective-permute-done((f32[16,384]{1,0:T(8,128)S(1)}, f32[16,384]{1,0:T(8,128)S(1)}, u32[]{:S(2)}, u32[]{:S(2)}) %collective-permute-start.9) | collective-permute-done | bytes 24608
  345.4 1.9 concatenate
  (33 shorter events, 8.6 us)
Async XLA Ops:
  7.2 70.1 %all-gather.5.cloned.1.call-start = ((), (), s32[]{:S(2)}) async-start(), calls=%async_computation.1 | async-start | bytes 11059200 | tf_op jit(solution)/shard_map/all_gather | solution.py:21
  7.9 105.4 %all-gather.3.cloned.1.call-start = ((), (), s32[]{:S(2)}) async-start(), calls=%async_computation | async-start | bytes 2764800 | tf_op jit(solution)/shard_map/all_gather | solution.py:20
  21.4 91.9 %copy-start = (bf16[1,1,197,768]{3,2,1,0:T(8,128)(2,1)S(1)}, bf16[1,1,197,768]{3,2,1,0:T(8,128)(2,1)}, u32[]{:S(2)}) copy-start(bf16[1,1,197,768]{3,2,1,0:T(8,128)(2,1)} %param.4) | copy-start | bytes 907780
  137.4 210.0 %copy-start.1 = (f32[12,384]{1,0:T(8,128)S(1)}, f32[12,384]{1,0:T(8,128)}, u32[]{:S(2)}) copy-start(f32[12,384]{1,0:T(8,128)} %param.7) | copy-start | bytes 55300
  279.9 25.1 %collective-permute-start.15 = (f32[12,384]{1,0:T(8,128)S(1)}, f32[12,384]{1,0:T(8,128)S(1)}, u32[]{:S(2)}, u32[]{:S(2)}) collective-permute-start(f32[12,384]{1,0:T(8,128)S(1)} %slice), channel_id=1, source_target_pairs={{0,128},{8,136},{16,144},{24,152},{32,160},{40,168},{48,176},{56,1... | collective-permute-start | bytes 55304
  288.3 24.7 %collective-permute-start = (f32[16,384]{1,0:T(8,128)S(1)}, f32[16,384]{1,0:T(8,128)S(1)}, u32[]{:S(2)}, u32[]{:S(2)}) collective-permute-start(f32[16,384]{1,0:T(8,128)S(1)} %fusion), channel_id=1, source_target_pairs={{0,8},{8,16},{16,24},{24,32},{32,40},{40,48},{48,56},{56,64},{64,7... | collective-permute-start | bytes 73736
  294.3 20.0 %collective-permute-start.1 = (f32[16,384]{1,0:T(8,128)S(1)}, f32[16,384]{1,0:T(8,128)S(1)}, u32[]{:S(2)}, u32[]{:S(2)}) collective-permute-start(f32[16,384]{1,0:T(8,128)S(1)} %fusion), channel_id=1, source_target_pairs={{0,16},{8,24},{16,32},{24,40},{32,48},{40,56},{48,64},{56,72},{64,... | collective-permute-start | bytes 73736
  300.0 15.5 %collective-permute-start.10 = (f32[16,384]{1,0:T(8,128)S(1)}, f32[16,384]{1,0:T(8,128)S(1)}, u32[]{:S(2)}, u32[]{:S(2)}) collective-permute-start(f32[16,384]{1,0:T(8,128)S(1)} %fusion), channel_id=1, source_target_pairs={{0,88},{8,96},{16,104},{24,112},{32,120},{40,128},{48,136},{56,144... | collective-permute-start | bytes 73736
  302.0 17.7 %collective-permute-start.11 = (f32[16,384]{1,0:T(8,128)S(1)}, f32[16,384]{1,0:T(8,128)S(1)}, u32[]{:S(2)}, u32[]{:S(2)}) collective-permute-start(f32[16,384]{1,0:T(8,128)S(1)} %fusion), channel_id=1, source_target_pairs={{0,96},{8,104},{16,112},{24,120},{32,128},{40,136},{48,144},{56,15... | collective-permute-start | bytes 73736
  305.1 17.3 %collective-permute-start.12 = (f32[16,384]{1,0:T(8,128)S(1)}, f32[16,384]{1,0:T(8,128)S(1)}, u32[]{:S(2)}, u32[]{:S(2)}) collective-permute-start(f32[16,384]{1,0:T(8,128)S(1)} %fusion), channel_id=1, source_target_pairs={{0,104},{8,112},{16,120},{24,128},{32,136},{40,144},{48,152},{56,1... | collective-permute-start | bytes 73736
  313.0 13.2 %collective-permute-start.13 = (f32[16,384]{1,0:T(8,128)S(1)}, f32[16,384]{1,0:T(8,128)S(1)}, u32[]{:S(2)}, u32[]{:S(2)}) collective-permute-start(f32[16,384]{1,0:T(8,128)S(1)} %fusion), channel_id=1, source_target_pairs={{0,112},{8,120},{16,128},{24,136},{32,144},{40,152},{48,160},{56,1... | collective-permute-start | bytes 73736
  314.3 14.3 %collective-permute-start.14 = (f32[16,384]{1,0:T(8,128)S(1)}, f32[16,384]{1,0:T(8,128)S(1)}, u32[]{:S(2)}, u32[]{:S(2)}) collective-permute-start(f32[16,384]{1,0:T(8,128)S(1)} %fusion), channel_id=1, source_target_pairs={{0,120},{8,128},{16,136},{24,144},{32,152},{40,160},{48,168},{56,1... | collective-permute-start | bytes 73736
  315.6 15.3 %collective-permute-start.2 = (f32[16,384]{1,0:T(8,128)S(1)}, f32[16,384]{1,0:T(8,128)S(1)}, u32[]{:S(2)}, u32[]{:S(2)}) collective-permute-start(f32[16,384]{1,0:T(8,128)S(1)} %fusion), channel_id=1, source_target_pairs={{0,24},{8,32},{16,40},{24,48},{32,56},{40,64},{48,72},{56,80},{64,... | collective-permute-start | bytes 73736
  319.6 13.2 %collective-permute-start.3 = (f32[16,384]{1,0:T(8,128)S(1)}, f32[16,384]{1,0:T(8,128)S(1)}, u32[]{:S(2)}, u32[]{:S(2)}) collective-permute-start(f32[16,384]{1,0:T(8,128)S(1)} %fusion), channel_id=1, source_target_pairs={{0,32},{8,40},{16,48},{24,56},{32,64},{40,72},{48,80},{56,88},{64,... | collective-permute-start | bytes 73736
  322.4 14.0 %collective-permute-start.4 = (f32[16,384]{1,0:T(8,128)S(1)}, f32[16,384]{1,0:T(8,128)S(1)}, u32[]{:S(2)}, u32[]{:S(2)}) collective-permute-start(f32[16,384]{1,0:T(8,128)S(1)} %fusion), channel_id=1, source_target_pairs={{0,40},{8,48},{16,56},{24,64},{32,72},{40,80},{48,88},{56,96},{64,... | collective-permute-start | bytes 73736
  326.2 14.1 %collective-permute-start.5 = (f32[16,384]{1,0:T(8,128)S(1)}, f32[16,384]{1,0:T(8,128)S(1)}, u32[]{:S(2)}, u32[]{:S(2)}) collective-permute-start(f32[16,384]{1,0:T(8,128)S(1)} %fusion), channel_id=1, source_target_pairs={{0,48},{8,56},{16,64},{24,72},{32,80},{40,88},{48,96},{56,104},{64... | collective-permute-start | bytes 73736
  328.6 11.7 %collective-permute-start.6 = (f32[16,384]{1,0:T(8,128)S(1)}, f32[16,384]{1,0:T(8,128)S(1)}, u32[]{:S(2)}, u32[]{:S(2)}) collective-permute-start(f32[16,384]{1,0:T(8,128)S(1)} %fusion), channel_id=1, source_target_pairs={{0,56},{8,64},{16,72},{24,80},{32,88},{40,96},{48,104},{56,112},{6... | collective-permute-start | bytes 73736
  330.9 9.4 %collective-permute-start.7 = (f32[16,384]{1,0:T(8,128)S(1)}, f32[16,384]{1,0:T(8,128)S(1)}, u32[]{:S(2)}, u32[]{:S(2)}) collective-permute-start(f32[16,384]{1,0:T(8,128)S(1)} %fusion), channel_id=1, source_target_pairs={{0,64},{8,72},{16,80},{24,88},{32,96},{40,104},{48,112},{56,120},{... | collective-permute-start | bytes 73736
  332.8 7.5 %collective-permute-start.8 = (f32[16,384]{1,0:T(8,128)S(1)}, f32[16,384]{1,0:T(8,128)S(1)}, u32[]{:S(2)}, u32[]{:S(2)}) collective-permute-start(f32[16,384]{1,0:T(8,128)S(1)} %fusion), channel_id=1, source_target_pairs={{0,72},{8,80},{16,88},{24,96},{32,104},{40,112},{48,120},{56,128},... | collective-permute-start | bytes 73736
  336.4 9.0 %collective-permute-start.9 = (f32[16,384]{1,0:T(8,128)S(1)}, f32[16,384]{1,0:T(8,128)S(1)}, u32[]{:S(2)}, u32[]{:S(2)}) collective-permute-start(f32[16,384]{1,0:T(8,128)S(1)} %fusion), channel_id=1, source_target_pairs={{0,80},{8,88},{16,96},{24,104},{32,112},{40,120},{48,128},{56,136}... | collective-permute-start | bytes 73736
Sparse Core Ops, SparseCore 0:
  10.1 67.1 all-gather.4
  79.4 33.7 all-gather.2
where the time goes:
time: 357 us; the launch traced here: 356 us
  blocking collectives  166 us (46%)
  waiting for transfers between devices  92.7 us (26%)
  starting transfers between devices  58.3 us (16%)
  between operations  18.8 us (5%)
  matrix products  13.3 us (4%)
  local copies, waits for them, and re-layouts  5.11 us (1%)
    unnamed x2, blocking collectives  152 us
    unnamed x16, starting transfers between devices  58.2 us
    all_gather x1, waiting for transfers between devices, per_device(): grad_piece = lax.all_gather(out_grads, 'aug', axis=1, tiled=True)  55.9 us
    all_gather x1, waiting for transfers between devices, per_device(): act_piece = lax.all_gather(activations, 'aug', axis=1, tiled=True)  30.2 us
    psum x1, blocking collectives, per_device(): square = lax.psum(gram_part * own_weight, 'aug')  14.5 us
  transfers between devices with their start and end apart: 18, of which 3 were waited for; matrix products, arithmetic and copies ran while one was open for 3% of the time, Pallas kernels for 0%

commit v1 on v0

v1 whole, which is shorter than its diff:
```python
import functools
import math

import jax
import jax.numpy as jnp
from jax import lax
from jax.experimental import pallas as pl
from jax.experimental.pallas import tpu as pltpu
from jax.sharding import PartitionSpec as P

MESH = pl.DeviceIdType.MESH
NZ, NX, NY = 16, 4, 4
S, D, FF = 197, 768, 3072
SP = 208
SLOT = 256
BW = FF // 8
CH = 3
CW = BW // CH
XR = D // NX
ZR = D // (NX * NZ)
HALF = 112
IMAGES = 64
CLIP = 0.01 * math.sqrt(D * FF * S)
LEVELS = 32766.0


def kernel(
    a_ref, g_ref, m_ref, n_ref,
    clip_ref, upd_ref, norm_ref,
    a_all, a_t, g_pad, g_all, perm, prod, x_in, parts, stat_out, stat_in, fac_out, fac_in, z_out, z_in,
    a_send, a_recv, g_send, g_recv, x_send, x_recv, s_send, s_recv, f_send, f_recv, z_send, z_recv, own_sem,
):
    img, aug = lax.axis_index("img"), lax.axis_index("aug")
    z, x, y, c = img // NX, lax.rem(img, NX), aug // 2, lax.rem(aug, 2)

    def at_y(dy, dc):
        return (img, lax.rem(y + dy, NY) * 2 + (lax.rem(c + dc, 2)))

    def at_x(dx):
        return (z * NX + lax.rem(x + dx, NX), aug)

    def at_z(dz):
        return (lax.rem(z + dz, NZ) * NX + x, aug)

    aug_peers = [(dy, dc) for dy in range(NY) for dc in range(2) if (dy, dc) != (0, 0)]

    barrier = pltpu.get_barrier_semaphore()
    for dy, dc in aug_peers:
        pl.semaphore_signal(barrier, inc=1, device_id=at_y(dy, dc), device_id_type=MESH)
    for dx in range(1, NX):
        pl.semaphore_signal(barrier, inc=1, device_id=at_x(dx), device_id_type=MESH)
    for dz in range(1, NZ):
        pl.semaphore_signal(barrier, inc=1, device_id=at_z(dz), device_id_type=MESH)

    mask = m_ref[...].astype(jnp.float32)
    tail = S - 192
    a_all[0:192, :] = (a_ref[0:192, :].astype(jnp.float32) * mask).astype(jnp.bfloat16)
    a_all[192:SLOT, :] = jnp.zeros((SLOT - 192, D), jnp.bfloat16)
    a_all[192:S, :] = (a_ref[192:S, :].astype(jnp.float32) * mask).astype(jnp.bfloat16)
    g_pad[0:192, :] = g_ref[0:192, :]
    g_pad[192:SP, :] = jnp.zeros((SP - 192, FF), jnp.bfloat16)
    g_pad[192:S, :] = g_ref[192:S, :]
    for s in range(8):
        if s:
            a_all[s * SLOT + SP:(s + 1) * SLOT, :] = jnp.zeros((SLOT - SP, D), jnp.bfloat16)
        g_all[s * SLOT + SP:(s + 1) * SLOT, :] = jnp.zeros((SLOT - SP, BW), jnp.bfloat16)

    p = lax.broadcasted_iota(jnp.int32, (D, 1), 0)
    px, pz, pr = p // XR, lax.rem(p, XR) // ZR, lax.rem(p, ZR)
    source = pz * (NX * ZR) + px * ZR + pr
    perm[...] = (lax.broadcasted_iota(jnp.int32, (D, D), 1) == source).astype(jnp.bfloat16)

    pl.semaphore_wait(barrier, 7 + (NX - 1) + (NZ - 1))

    def a_copy(i, src, dst, rows, device):
        return pltpu.make_async_remote_copy(
            src_ref=a_all.at[pl.ds(src, rows)], dst_ref=a_all.at[pl.ds(dst, rows)],
            send_sem=a_send.at[i], recv_sem=a_recv.at[i], device_id=device, device_id_type=MESH)

    def slot(dy, dc):
        return (dy * 2 + dc) * SLOT

    up = a_copy(0, 0, slot(1, 0), SP, at_y(1, 0))
    down = a_copy(1, 0, slot(3, 0), SP, at_y(3, 0))
    side = a_copy(2, 0, slot(0, 1), SP, at_y(0, 1))
    up.start()
    down.start()
    side.start()

    own_block = pl.ds(pl.multiple_of(aug * BW, BW), BW)
    own_copy = pltpu.make_async_copy(g_pad.at[:, own_block], g_all.at[pl.ds(0, SP)], own_sem)
    own_copy.start()

    g_copies = [[] for _ in range(CH)]

    def start_g(k):
        for i, (dy, dc) in enumerate([(1, 0), (3, 0), (1, 1), (3, 1), (2, 0), (2, 1), (0, 1)]):
            to = lax.rem(y + dy, NY) * 2 + lax.rem(c + dc, 2)
            copy = pltpu.make_async_remote_copy(
                src_ref=g_pad.at[:, pl.ds(pl.multiple_of(to * BW + k * CW, CW), CW)],
                dst_ref=g_all.at[pl.ds(slot(dy, dc), SP), pl.ds(k * CW, CW)],
                send_sem=g_send.at[k, i], recv_sem=g_recv.at[k, i], device_id=at_y(dy, dc), device_id_type=MESH)
            copy.start()
            g_copies[k].append(copy)

    def transpose(s):
        a_t[:, s * SLOT:(s + 1) * SLOT] = lax.dot_general(
            perm[...], a_all[s * SLOT:(s + 1) * SLOT, :], (((1,), (1,)), ((), ())),
            preferred_element_type=jnp.float32).astype(jnp.bfloat16)

    start_g(0)
    transpose(0)
    up.wait_recv()
    far_up = a_copy(3, slot(1, 0), slot(2, 0), HALF, at_y(1, 0))
    far_up.start()
    side_up = a_copy(4, slot(1, 0), slot(1, 1), SP, at_y(0, 1))
    side_up.start()
    down.wait_recv()
    far_down = a_copy(5, slot(3, 0) + HALF, slot(2, 0) + HALF, SP - HALF, at_y(3, 0))
    far_down.start()
    side_down = a_copy(6, slot(3, 0), slot(3, 1), SP, at_y(0, 1))
    side_down.start()
    start_g(1)
    start_g(2)
    side.wait_recv()
    transpose(1)
    transpose(2)
    transpose(6)
    far_up.wait_recv()
    far_down.wait_recv()
    side_far = a_copy(7, slot(2, 0), slot(2, 1), SP, at_y(0, 1))
    side_far.start()
    transpose(4)
    side_up.wait_recv()
    transpose(3)
    side_down.wait_recv()
    transpose(7)
    side_far.wait_recv()
    transpose(5)
    own_copy.wait()

    x_copies = [[] for _ in range(CH)]
    total = jnp.zeros((1, CW), jnp.float32)
    for k in range(CH):
        for copy in g_copies[k]:
            copy.wait_recv()
        cols = slice(k * CW, (k + 1) * CW)
        block = jnp.dot(a_t[...], g_all[:, cols], preferred_element_type=jnp.float32)
        prod[:, cols] = block
        for dx in range(1, NX):
            to = lax.rem(x + dx, NX)
            copy = pltpu.make_async_remote_copy(
                src_ref=prod.at[pl.ds(pl.multiple_of(to * XR, XR), XR), pl.ds(k * CW, CW)],
                dst_ref=x_in.at[dx - 1, :, pl.ds(k * CW, CW)],
                send_sem=x_send.at[k, dx - 1], recv_sem=x_recv.at[k, dx - 1], device_id=at_x(dx), device_id_type=MESH)
            copy.start()
            x_copies[k].append(copy)
        total = total + jnp.sum(block * block, axis=0, keepdims=True)

    square = jnp.sum(total, axis=1, keepdims=True)
    row = lax.broadcasted_iota(jnp.int32, (8, 128), 0)
    stat = jnp.where(row < 4, jnp.broadcast_to(square, (8, 128)), jnp.broadcast_to(mask, (8, 128)))
    stat_out[...] = stat
    s_copies = []
    for i, (dy, dc) in enumerate(aug_peers):
        copy = pltpu.make_async_remote_copy(
            src_ref=stat_out, dst_ref=stat_in.at[i], send_sem=s_send.at[i], recv_sem=s_recv.at[i],
            device_id=at_y(dy, dc), device_id_type=MESH)
        copy.start()
        s_copies.append(copy)
    for copy in s_copies:
        copy.wait_recv()
    near = (stat + stat_in[0]) + (stat_in[3] + stat_in[4])
    far = (stat_in[1] + stat_in[2]) + (stat_in[5] + stat_in[6])
    stat = near + far
    count = stat[4:5, :]
    norm = jnp.sqrt(stat[0:1, :]) / count
    factor = CLIP / jnp.maximum(norm, CLIP)
    weight = factor / count
    norm_ref[...] = norm[:, 0:1]
    fac_out[...] = jnp.broadcast_to(weight, (8, 128))
    f_copies = []
    for dx in range(1, NX):
        copy = pltpu.make_async_remote_copy(
            src_ref=fac_out, dst_ref=fac_in.at[dx - 1], send_sem=f_send.at[dx - 1], recv_sem=f_recv.at[dx - 1],
            device_id=at_x(dx), device_id_type=MESH)
        copy.start()
        f_copies.append(copy)

    own_rows = pl.ds(pl.multiple_of(x * XR, XR), XR)
    for k in range(CH):
        cols = slice(k * CW, (k + 1) * CW)
        parts[:, cols] = weight * prod[own_rows, cols]
    for dx in range(1, NX):
        f_copies[dx - 1].wait_recv()
        far = fac_in[dx - 1, 0:1, :]
        for k in range(CH):
            x_copies[k][dx - 1].wait_recv()
            cols = slice(k * CW, (k + 1) * CW)
            parts[:, cols] += far * x_in[dx - 1, :, cols]

    def scale_of(level):
        return jnp.exp2(level.astype(jnp.float32) * (1.0 / 64.0))

    row8 = lax.broadcasted_iota(jnp.int32, (8, BW), 0)
    for d in range(NZ):
        piece = parts[d * ZR:(d + 1) * ZR, :]
        top = jnp.maximum(jnp.max(jnp.abs(piece), axis=0, keepdims=True), 1e-30)
        level = jnp.ceil(jnp.log2(top) * 64.0).astype(jnp.int32) + 1
        ints = jnp.round(piece * (LEVELS / scale_of(level))).astype(jnp.int32)
        z_out[d, 0:6, :] = ints[0:6] * 65536 + ints[6:12]
        z_out[d, 6:8, :] = jnp.broadcast_to(level, (2, BW))
    z_copies = []
    for d in range(1, NZ):
        copy = pltpu.make_async_remote_copy(
            src_ref=z_out.at[lax.rem(z + d, NZ)], dst_ref=z_in.at[d - 1], send_sem=z_send.at[d - 1], recv_sem=z_recv.at[d - 1],
            device_id=at_z(d), device_id_type=MESH)
        copy.start()
        z_copies.append(copy)

    def unpack(words):
        high = (words[0:6] + 32768) >> 16
        low = words[0:6] - high * 65536
        scale = scale_of(words[6:7]) * (1.0 / LEVELS)
        return high.astype(jnp.float32) * scale, low.astype(jnp.float32) * scale

    top_rows, low_rows = unpack(z_out[z])
    for d in range(1, NZ):
        z_copies[d - 1].wait_recv()
        one, two = unpack(z_in[d - 1])
        top_rows = top_rows + one
        low_rows = low_rows + two
    clip_ref[0:6, :] = top_rows
    clip_ref[6:12, :] = low_rows
    clipped = clip_ref[...]
    upd_ref[...] = (clipped + CLIP * n_ref[...]) * (1.0 / IMAGES)

    for copy in [up, down, side, far_up, side_up, far_down, side_down, side_far]:
        copy.wait_send()
    for copy in sum(g_copies, []) + sum(x_copies, []) + s_copies + f_copies + z_copies:
        copy.wait_send()


def per_device(activations, out_grads, kept_mask, noise_field):
    vmem = pl.BlockSpec(memory_space=pltpu.VMEM)
    dma = pltpu.SemaphoreType.DMA
    bf16, f32 = jnp.bfloat16, jnp.float32
    clipped, update, norm = pl.pallas_call(
        kernel,
        out_shape=(
            jax.ShapeDtypeStruct((ZR, BW), f32), jax.ShapeDtypeStruct((ZR, BW), f32), jax.ShapeDtypeStruct((1, 1), f32)),
        in_specs=[vmem] * 4,
        out_specs=(vmem,) * 3,
        scratch_shapes=[
            pltpu.VMEM((8 * SLOT, D), bf16),
            pltpu.VMEM((D, 8 * SLOT), bf16),
            pltpu.VMEM((SP, FF), bf16),
            pltpu.VMEM((8 * SLOT, BW), bf16),
            pltpu.VMEM((D, D), bf16),
            pltpu.VMEM((D, BW), f32),
            pltpu.VMEM((NX - 1, XR, BW), f32),
            pltpu.VMEM((XR, BW), f32),
            pltpu.VMEM((8, 128), f32),
            pltpu.VMEM((7, 8, 128), f32),
            pltpu.VMEM((8, 128), f32),
            pltpu.VMEM((NX - 1, 8, 128), f32),
            pltpu.VMEM((NZ, 8, BW), jnp.int32),
            pltpu.VMEM((NZ - 1, 8, BW), jnp.int32),
            dma((8,)), dma((8,)), dma((CH, 7)), dma((CH, 7)), dma((CH, NX - 1)), dma((CH, NX - 1)),
            dma((7,)), dma((7,)), dma((NX - 1,)), dma((NX - 1,)), dma((NZ - 1,)), dma((NZ - 1,)), dma,
        ],
        compiler_params=pltpu.CompilerParams(collective_id=0, has_side_effects=True, vmem_limit_bytes=40 * 2**20),
        name="clipped_sum",
    )(activations[0, 0], out_grads[0, 0], kept_mask, noise_field)
    return clipped, update, norm.reshape(1)


def solution(mesh):
    in_specs = (
        P("img", "aug", None, None),
        P("img", "aug", None, None),
        P("img", "aug"),
        P("img", "aug"),
    )
    out_specs = (P("img", "aug"), P("img", "aug"), P("img"))
    return jax.shard_map(
        per_device, mesh=mesh, in_specs=in_specs, out_specs=out_specs, check_vma=False
    )
```

time: 357 us -> 73.4 us (0.21)
  the two profiles are of different devices: /device:TPU:70 before, /device:TPU:2 now
where the time goes in v1:
time: 73.4 us; the launch traced here: 73.1 us
  Pallas kernels  65.8 us (90%)
  local copies, waits for them, and re-layouts  4.2 us (6%)
  between operations  3.03 us (4%)
    pallas_call x1, Pallas kernels, per_device(): pl.pallas_call(kernel, out_shape=(jax.ShapeDtypeStruct((ZR, BW), f32), ja...  65.8 us
    unnamed x8, local copies, waits for them, and re-layouts  4.2 us

profile of v1, /device:TPU:2, one launch (start us, length us, event | category | flops | bytes accessed | tf_op | source)
XLA Modules:
  0.0 73.1 jit_solution(5307617275695071383)
XLA Ops:
  1.3 0.0 copy-start
  1.3 1.3 %copy-done = bf16[1,1,197,3072]{3,2,1,0:T(8,128)(2,1)S(1)} copy-done((bf16[1,1,197,3072]{3,2,1,0:T(8,128)(2,1)S(1)}, bf16[1,1,197,3072]{3,2,1,0:T(8,128)(2,1)}, u32[]{:S(2)}) %copy-start) | copy-done | bytes 1210392
  2.6 0.0 copy-start.1
  2.6 1.0 %copy-done.1 = bf16[1,1,197,768]{3,2,1,0:T(8,128)(2,1)S(1)} copy-done((bf16[1,1,197,768]{3,2,1,0:T(8,128)(2,1)S(1)}, bf16[1,1,197,768]{3,2,1,0:T(8,128)(2,1)}, u32[]{:S(2)}) %copy-start.1) | copy-done | bytes 302616
  3.5 0.0 copy-start.2
  3.5 0.7 %copy-done.2 = f32[12,384]{1,0:T(8,128)S(1)} copy-done((f32[12,384]{1,0:T(8,128)S(1)}, f32[12,384]{1,0:T(8,128)}, u32[]{:S(2)}) %copy-start.2) | copy-done | bytes 18456
  4.3 65.8 %clipped_sum.1 = (f32[12,384]{1,0:T(8,128)S(1)}, f32[12,384]{1,0:T(8,128)S(1)}, f32[1,1]{1,0:T(1,128)}) custom-call(bf16[197,768]{1,0:T(8,128)(2,1)S(1)} %bitcast.4, bf16[197,3072]{1,0:T(8,128)(2,1)S(1)} %bitcast.3, s32[1,1]{1,0:T(1,128)S(6)} %copy.10.m_ref, f32[12,384]{1,0:T(8,128)S(1)} %copy-done.2), custom_call_target="tpu_custom_call" | custom-call | tf_op jit(solution)/shard_map/clipped_sum/pallas_call | solution.py:248
  70.1 0.6 copy.11
  70.7 0.6 copy.12
Async XLA Ops:
  1.3 1.3 %copy-start = (bf16[1,1,197,3072]{3,2,1,0:T(8,128)(2,1)S(1)}, bf16[1,1,197,3072]{3,2,1,0:T(8,128)(2,1)}, u32[]{:S(2)}) copy-start(bf16[1,1,197,3072]{3,2,1,0:T(8,128)(2,1)} %param.5) | copy-start | bytes 3631108
  2.6 1.0 %copy-start.1 = (bf16[1,1,197,768]{3,2,1,0:T(8,128)(2,1)S(1)}, bf16[1,1,197,768]{3,2,1,0:T(8,128)(2,1)}, u32[]{:S(2)}) copy-start(bf16[1,1,197,768]{3,2,1,0:T(8,128)(2,1)} %param.4) | copy-start | bytes 907780
  3.5 0.7 %copy-start.2 = (f32[12,384]{1,0:T(8,128)S(1)}, f32[12,384]{1,0:T(8,128)}, u32[]{:S(2)}) copy-start(f32[12,384]{1,0:T(8,128)} %n_ref.1) | copy-start | bytes 55300

commit v2 on v1

v2 whole, which is shorter than its diff:
```python
import functools
import math

import jax
import jax.numpy as jnp
from jax import lax
from jax.experimental import pallas as pl
from jax.experimental.pallas import tpu as pltpu
from jax.sharding import PartitionSpec as P

MESH = pl.DeviceIdType.MESH
NZ, NX, NY = 16, 4, 4
S, D, FF = 197, 768, 3072
SP = 208
BW = FF // 8
CH = 3
CW = BW // CH
XR = D // NX
ZR = D // (NX * NZ)
HALF = 112
IMAGES = 64
CLIP = 0.01 * math.sqrt(D * FF * S)
LEVELS = 32766.0


def kernel(
    a_hbm, g_hbm, m_ref, n_hbm,
    clip_ref, upd_ref, norm_ref,
    a_raw, g_raw, noise, a_all, a_perm, g_pad, g_all, perm, prod, x_out, x_in, parts,
    stat_out, stat_in, fac_out, fac_in, z_out, z_in,
    in_sem, a_send, a_recv, g_send, g_recv, x_send, x_recv, s_send, s_recv, f_send, f_recv, z_send, z_recv, own_sem,
):
    img, aug = lax.axis_index("img"), lax.axis_index("aug")
    z, x, y, c = img // NX, lax.rem(img, NX), aug // 2, lax.rem(aug, 2)

    def at_y(dy, dc):
        return (img, lax.rem(y + dy, NY) * 2 + (lax.rem(c + dc, 2)))

    def at_x(dx):
        return (z * NX + lax.rem(x + dx, NX), aug)

    def at_z(dz):
        return (lax.rem(z + dz, NZ) * NX + x, aug)

    aug_peers = [(dy, dc) for dy in range(NY) for dc in range(2) if (dy, dc) != (0, 0)]

    barrier = pltpu.get_barrier_semaphore()
    for dy, dc in aug_peers:
        pl.semaphore_signal(barrier, inc=1, device_id=at_y(dy, dc), device_id_type=MESH)
    for dx in range(1, NX):
        pl.semaphore_signal(barrier, inc=1, device_id=at_x(dx), device_id_type=MESH)
    for dz in range(1, NZ):
        pl.semaphore_signal(barrier, inc=1, device_id=at_z(dz), device_id_type=MESH)

    a_load = pltpu.make_async_copy(a_hbm, a_raw, in_sem.at[0])
    g_load = pltpu.make_async_copy(g_hbm, g_raw, in_sem.at[1])
    n_load = pltpu.make_async_copy(n_hbm, noise, in_sem.at[2])
    a_load.start()
    g_load.start()
    n_load.start()

    p = lax.broadcasted_iota(jnp.int32, (1, D), 1)
    px, pz, pr = p // XR, lax.rem(p, XR) // ZR, lax.rem(p, ZR)
    source = pz * (NX * ZR) + px * ZR + pr
    perm[...] = (lax.broadcasted_iota(jnp.int32, (D, D), 0) == source).astype(jnp.bfloat16)

    mask = m_ref[...].astype(jnp.float32)
    a_load.wait()
    a_all[0:192, :] = (a_raw[0:192, :].astype(jnp.float32) * mask).astype(jnp.bfloat16)
    a_all[192:SP, :] = jnp.zeros((SP - 192, D), jnp.bfloat16)
    a_all[192:S, :] = (a_raw[192:S, :].astype(jnp.float32) * mask).astype(jnp.bfloat16)

    pl.semaphore_wait(barrier, 7 + (NX - 1) + (NZ - 1))

    def a_copy(i, src, dst, first, rows, device):
        return pltpu.make_async_remote_copy(
            src_ref=a_all.at[pl.ds(src * SP + first, rows)], dst_ref=a_all.at[pl.ds(dst * SP + first, rows)],
            send_sem=a_send.at[i], recv_sem=a_recv.at[i], device_id=device, device_id_type=MESH)

    up_far = a_copy(0, 0, 2, 0, HALF, at_y(1, 0))
    down_far = a_copy(1, 0, 6, HALF, SP - HALF, at_y(3, 0))
    up_near = a_copy(2, 0, 2, HALF, SP - HALF, at_y(1, 0))
    down_near = a_copy(3, 0, 6, 0, HALF, at_y(3, 0))
    side = a_copy(4, 0, 1, 0, SP, at_y(0, 1))
    a_copies = [up_far, down_far, up_near, down_near, side]
    for copy in a_copies:
        copy.start()

    g_load.wait()
    g_pad[0:192, :] = g_raw[0:192, :]
    g_pad[192:SP, :] = jnp.zeros((SP - 192, FF), jnp.bfloat16)
    g_pad[192:S, :] = g_raw[192:S, :]
    own_block = pl.ds(pl.multiple_of(aug * BW, BW), BW)
    own_copy = pltpu.make_async_copy(g_pad.at[:, own_block], g_all.at[pl.ds(0, SP)], own_sem)
    own_copy.start()

    up_far.wait_recv()
    far_up = a_copy(5, 2, 4, 0, HALF, at_y(1, 0))
    far_up.start()
    down_far.wait_recv()
    far_down = a_copy(6, 6, 4, HALF, SP - HALF, at_y(3, 0))
    far_down.start()

    g_copies = [[] for _ in range(CH)]
    for k in range(CH):
        for i, (dy, dc) in enumerate([(1, 0), (3, 0), (1, 1), (3, 1), (2, 0), (2, 1), (0, 1)]):
            to = lax.rem(y + dy, NY) * 2 + lax.rem(c + dc, 2)
            copy = pltpu.make_async_remote_copy(
                src_ref=g_pad.at[:, pl.ds(pl.multiple_of(to * BW + k * CW, CW), CW)],
                dst_ref=g_all.at[pl.ds((dy * 2 + dc) * SP, SP), pl.ds(k * CW, CW)],
                send_sem=g_send.at[k, i], recv_sem=g_recv.at[k, i], device_id=at_y(dy, dc), device_id_type=MESH)
            copy.start()
            g_copies[k].append(copy)

    def permute(s):
        rows = slice(s * SP, (s + 1) * SP)
        a_perm[rows, :] = jnp.dot(a_all[rows, :], perm[...], preferred_element_type=jnp.float32).astype(jnp.bfloat16)

    up_near.wait_recv()
    side_up = a_copy(7, 2, 3, 0, SP, at_y(0, 1))
    side_up.start()
    down_near.wait_recv()
    side_down = a_copy(8, 6, 7, 0, SP, at_y(0, 1))
    side_down.start()
    permute(0)
    side.wait_recv()
    permute(1)
    permute(2)
    permute(6)
    far_up.wait_recv()
    far_down.wait_recv()
    side_far = a_copy(9, 4, 5, 0, SP, at_y(0, 1))
    side_far.start()
    permute(4)
    side_up.wait_recv()
    permute(3)
    side_down.wait_recv()
    permute(7)
    side_far.wait_recv()
    permute(5)
    a_copies += [far_up, far_down, side_up, side_down, side_far]
    own_copy.wait()

    def scale_of(level):
        return jnp.exp2(level.astype(jnp.float32) * (1.0 / 64.0))

    def pack(piece):
        half = piece.shape[0] // 2
        top = jnp.maximum(jnp.max(jnp.abs(piece), axis=0, keepdims=True), 1e-30)
        level = jnp.ceil(jnp.log2(top) * 64.0).astype(jnp.int32) + 1
        ints = jnp.round(piece * (LEVELS / scale_of(level))).astype(jnp.int32)
        return ints[:half] * 65536 + ints[half:], level

    def unpack(words, level, weight):
        high = (words + 32768) >> 16
        low = words - high * 65536
        scale = scale_of(level) * (weight * (1.0 / LEVELS))
        return high.astype(jnp.float32) * scale, low.astype(jnp.float32) * scale

    x_copies = [[] for _ in range(CH)]
    total = jnp.zeros((1, CW), jnp.float32)
    for k in range(CH):
        for copy in g_copies[k]:
            copy.wait_recv()
        cols = slice(k * CW, (k + 1) * CW)
        block = lax.dot_general(
            a_perm[...], g_all[:, cols], (((0,), (0,)), ((), ())), preferred_element_type=jnp.float32)
        prod[:, cols] = block
        for t in range(NX):
            words, level = pack(block[t * XR:(t + 1) * XR])
            x_out[k, t, 0:XR // 2, :] = words
            x_out[k, t, XR // 2:, :] = jnp.broadcast_to(level, (8, CW))
        for dx in range(1, NX):
            copy = pltpu.make_async_remote_copy(
                src_ref=x_out.at[k, lax.rem(x + dx, NX)], dst_ref=x_in.at[k, dx - 1],
                send_sem=x_send.at[k, dx - 1], recv_sem=x_recv.at[k, dx - 1], device_id=at_x(dx), device_id_type=MESH)
            copy.start()
            x_copies[k].append(copy)
        total = total + jnp.sum(block * block, axis=0, keepdims=True)

    square = jnp.sum(total, axis=1, keepdims=True)
    row = lax.broadcasted_iota(jnp.int32, (8, 128), 0)
    stat = jnp.where(row < 4, jnp.broadcast_to(square, (8, 128)), jnp.broadcast_to(mask, (8, 128)))
    stat_out[...] = stat
    s_copies = []
    for i, (dy, dc) in enumerate(aug_peers):
        copy = pltpu.make_async_remote_copy(
            src_ref=stat_out, dst_ref=stat_in.at[i], send_sem=s_send.at[i], recv_sem=s_recv.at[i],
            device_id=at_y(dy, dc), device_id_type=MESH)
        copy.start()
        s_copies.append(copy)
    for copy in s_copies:
        copy.wait_recv()
    near = (stat + stat_in[0]) + (stat_in[3] + stat_in[4])
    far = (stat_in[1] + stat_in[2]) + (stat_in[5] + stat_in[6])
    stat = near + far
    count = stat[4:5, :]
    norm = jnp.sqrt(stat[0:1, :]) / count
    factor = CLIP / jnp.maximum(norm, CLIP)
    weight = factor / count
    norm_ref[...] = norm[:, 0:1]
    fac_out[...] = jnp.broadcast_to(weight, (8, 128))
    f_copies = []
    for dx in range(1, NX):
        copy = pltpu.make_async_remote_copy(
            src_ref=fac_out, dst_ref=fac_in.at[dx - 1], send_sem=f_send.at[dx - 1], recv_sem=f_recv.at[dx - 1],
            device_id=at_x(dx), device_id_type=MESH)
        copy.start()
        f_copies.append(copy)

    own_rows = pl.ds(pl.multiple_of(x * XR, XR), XR)
    for k in range(CH):
        cols = slice(k * CW, (k + 1) * CW)
        parts[:, cols] = weight * prod[own_rows, cols]
    for copy in f_copies:
        copy.wait_recv()
    half = XR // 2
    for k in range(CH):
        cols = slice(k * CW, (k + 1) * CW)
        high, low = parts[0:half, cols], parts[half:, cols]
        for d in range(NX - 1):
            x_copies[k][d].wait_recv()
            one, two = unpack(x_in[k, d, 0:half, :], x_in[k, d, half:half + 1, :], fac_in[d, 0:1, :])
            high = high + one
            low = low + two
        parts[0:half, cols] = high
        parts[half:, cols] = low

    for d in range(NZ):
        words, level = pack(parts[d * ZR:(d + 1) * ZR, :])
        z_out[d, 0:6, :] = words
        z_out[d, 6:8, :] = jnp.broadcast_to(level, (2, BW))
    z_copies = []
    for d in range(1, NZ):
        copy = pltpu.make_async_remote_copy(
            src_ref=z_out.at[lax.rem(z + d, NZ)], dst_ref=z_in.at[d - 1], send_sem=z_send.at[d - 1], recv_sem=z_recv.at[d - 1],
            device_id=at_z(d), device_id_type=MESH)
        copy.start()
        z_copies.append(copy)

    own = z_out[z]
    top_rows, low_rows = unpack(own[0:6], own[6:7], 1.0)
    for d in range(1, NZ):
        z_copies[d - 1].wait_recv()
        words = z_in[d - 1]
        one, two = unpack(words[0:6], words[6:7], 1.0)
        top_rows = top_rows + one
        low_rows = low_rows + two
    n_load.wait()
    clip_ref[0:6, :] = top_rows
    clip_ref[6:12, :] = low_rows
    upd_ref[0:6, :] = (top_rows + CLIP * noise[0:6, :]) * (1.0 / IMAGES)
    upd_ref[6:12, :] = (low_rows + CLIP * noise[6:12, :]) * (1.0 / IMAGES)

    for copy in a_copies + sum(g_copies, []) + sum(x_copies, []) + s_copies + f_copies + z_copies:
        copy.wait_send()


def per_device(activations, out_grads, kept_mask, noise_field):
    vmem = pl.BlockSpec(memory_space=pltpu.VMEM)
    hbm = pl.BlockSpec(memory_space=pl.ANY)
    dma = pltpu.SemaphoreType.DMA
    bf16, f32, i32 = jnp.bfloat16, jnp.float32, jnp.int32
    clipped, update, norm = pl.pallas_call(
        kernel,
        out_shape=(
            jax.ShapeDtypeStruct((ZR, BW), f32), jax.ShapeDtypeStruct((ZR, BW), f32), jax.ShapeDtypeStruct((1, 1), f32)),
        in_specs=[hbm, hbm, vmem, hbm],
        out_specs=(vmem,) * 3,
        scratch_shapes=[
            pltpu.VMEM((S, D), bf16),
            pltpu.VMEM((S, FF), bf16),
            pltpu.VMEM((ZR, BW), f32),
            pltpu.VMEM((8 * SP, D), bf16),
            pltpu.VMEM((8 * SP, D), bf16),
            pltpu.VMEM((SP, FF), bf16),
            pltpu.VMEM((8 * SP, BW), bf16),
            pltpu.VMEM((D, D), bf16),
            pltpu.VMEM((D, BW), f32),
            pltpu.VMEM((CH, NX, XR // 2 + 8, CW), i32),
            pltpu.VMEM((CH, NX - 1, XR // 2 + 8, CW), i32),
            pltpu.VMEM((XR, BW), f32),
            pltpu.VMEM((8, 128), f32),
            pltpu.VMEM((7, 8, 128), f32),
            pltpu.VMEM((8, 128), f32),
            pltpu.VMEM((NX - 1, 8, 128), f32),
            pltpu.VMEM((NZ, 8, BW), i32),
            pltpu.VMEM((NZ - 1, 8, BW), i32),
            dma((3,)), dma((10,)), dma((10,)), dma((CH, 7)), dma((CH, 7)), dma((CH, NX - 1)), dma((CH, NX - 1)),
            dma((7,)), dma((7,)), dma((NX - 1,)), dma((NX - 1,)), dma((NZ - 1,)), dma((NZ - 1,)), dma,
        ],
        compiler_params=pltpu.CompilerParams(collective_id=0, has_side_effects=True, vmem_limit_bytes=56 * 2**20),
        name="clipped_sum",
    )(activations[0, 0], out_grads[0, 0], kept_mask, noise_field)
    return clipped, update, norm.reshape(1)


def solution(mesh):
    in_specs = (
        P("img", "aug", None, None),
        P("img", "aug", None, None),
        P("img", "aug"),
        P("img", "aug"),
    )
    out_specs = (P("img", "aug"), P("img", "aug"), P("img"))
    return jax.shard_map(
        per_device, mesh=mesh, in_specs=in_specs, out_specs=out_specs, check_vma=False
    )
```

time: 73.4 us -> 68.7 us (0.936)
  the two profiles are of different devices: /device:TPU:2 before, /device:TPU:1 now
where the time goes in v2:
time: 68.7 us; the launch traced here: 67.4 us
  Pallas kernels  61.6 us (90%)
  between operations  3.03 us (4%)
  local copies, waits for them, and re-layouts  2.69 us (4%)
    pallas_call x1, Pallas kernels, per_device(): pl.pallas_call(kernel, out_shape=(jax.ShapeDtypeStruct((ZR, BW), f32), ja...  61.6 us
    unnamed x2, local copies, waits for them, and re-layouts  2.69 us

profile of v2, /device:TPU:1, one launch (start us, length us, event | category | flops | bytes accessed | tf_op | source)
XLA Modules:
  0.0 67.4 jit_solution(11152364744543346816)
XLA Ops:
  1.3 61.6 %clipped_sum.1 = (f32[12,384]{1,0:T(8,128)}, f32[12,384]{1,0:T(8,128)}, f32[1,1]{1,0:T(1,128)}) custom-call(bf16[197,768]{1,0:T(8,128)(2,1)} %bitcast.4, bf16[197,3072]{1,0:T(8,128)(2,1)} %bitcast.3, s32[1,1]{1,0:T(1,128)S(6)} %copy.10.m_ref, f32[12,384]{1,0:T(8,128)} %n_hbm.1), custom_call_target="tpu_custom_call" | custom-call | tf_op jit(solution)/shard_map/clipped_sum/pallas_call | solution.py:264
  62.9 1.3 %copy.11 = f32[12,384]{1,0:T(8,128)} copy(f32[12,384]{1,0:T(8,128)} %get-tuple-element.12) | data formatting | bytes 36864
  64.3 1.3 %copy.12 = f32[12,384]{1,0:T(8,128)} copy(f32[12,384]{1,0:T(8,128)} %get-tuple-element.13) | data formatting | bytes 36864

commit v3 on v2

v3 whole, which is shorter than its diff:
```python
import functools
import math

import jax
import jax.numpy as jnp
from jax import lax
from jax.experimental import pallas as pl
from jax.experimental.pallas import tpu as pltpu
from jax.sharding import PartitionSpec as P

MESH = pl.DeviceIdType.MESH
NZ, NX, NY = 16, 4, 4
S, D, FF = 197, 768, 3072
SP = 208
BW = FF // 8
CH = 3
CW = BW // CH
XR = D // NX
ZR = D // (NX * NZ)
HALF = 112
IMAGES = 64
CLIP = 0.01 * math.sqrt(D * FF * S)
LEVELS = 32766.0
X_ORDER = (2, 1, 3, 0)
Z_ORDER = (8, 7, 9, 6, 10, 5, 11, 4, 12, 3, 13, 2, 14, 1, 15, 0)


def kernel(
    a_hbm, g_hbm, m_ref,
    own_ref, rest_ref, norm_ref,
    a_raw, g_raw, a_all, a_perm, g_pad, g_all, perm, own_part, x_out, x_in, parts,
    stat_out, stat_in, fac_out, fac_in, z_out, z_in,
    in_sem, a_send, a_recv, g_send, g_recv, x_send, x_recv, s_send, s_recv, f_send, f_recv, z_send, z_recv, own_sem, met,
):
    img, aug = lax.axis_index("img"), lax.axis_index("aug")
    z, x, y, c = img // NX, lax.rem(img, NX), aug // 2, lax.rem(aug, 2)

    def at_y(dy, dc):
        return (img, lax.rem(y + dy, NY) * 2 + (lax.rem(c + dc, 2)))

    def at_x(dx):
        return (z * NX + lax.rem(x + dx, NX), aug)

    def at_z(dz):
        return (lax.rem(z + dz + NZ, NZ) * NX + x, aug)

    same_core = [(1, 0), (3, 0), (2, 0)]
    other_core = [(0, 1), (1, 1), (3, 1), (2, 1)]
    aug_peers = [(dy, dc) for dy in range(NY) for dc in range(2) if (dy, dc) != (0, 0)]

    barrier = pltpu.get_barrier_semaphore()
    for dy, dc in aug_peers:
        pl.semaphore_signal(barrier, inc=1, device_id=at_y(dy, dc), device_id_type=MESH)
    for dx in range(1, NX):
        pl.semaphore_signal(barrier, inc=1, device_id=at_x(dx), device_id_type=MESH)
    for dz in (1, -1):
        pl.semaphore_signal(barrier, inc=1, device_id=at_z(dz), device_id_type=MESH)

    a_load = pltpu.make_async_copy(a_hbm, a_raw, in_sem.at[0])
    g_load = pltpu.make_async_copy(g_hbm, g_raw, in_sem.at[1])
    a_load.start()
    g_load.start()

    p = lax.broadcasted_iota(jnp.int32, (1, D), 1)
    px, pz, pr = p // XR, lax.rem(p, XR) // ZR, lax.rem(p, ZR)
    to_x = lax.rem(x + jnp.where(px == 0, 2, jnp.where(px == 3, 0, px * 2 - 1)), NX)
    source = lax.rem(z + pz, NZ) * (NX * ZR) + to_x * ZR + pr
    perm[...] = (lax.broadcasted_iota(jnp.int32, (D, D), 0) == source).astype(jnp.bfloat16)

    mask = m_ref[...].astype(jnp.float32)
    a_load.wait()
    a_all[0:192, :] = (a_raw[0:192, :].astype(jnp.float32) * mask).astype(jnp.bfloat16)
    a_all[192:SP, :] = jnp.zeros((SP - 192, D), jnp.bfloat16)
    a_all[192:S, :] = (a_raw[192:S, :].astype(jnp.float32) * mask).astype(jnp.bfloat16)

    pl.semaphore_wait(barrier, 7 + (NX - 1) + 2)

    def call_z(step):
        for dz in (1 << step, -(1 << step)):
            pl.semaphore_signal(met.at[step], inc=1, device_id=at_z(dz), device_id_type=MESH)

    call_z(0)

    def a_copy(i, src, dst, first, rows, device):
        return pltpu.make_async_remote_copy(
            src_ref=a_all.at[pl.ds(src * SP + first, rows)], dst_ref=a_all.at[pl.ds(dst * SP + first, rows)],
            send_sem=a_send.at[i], recv_sem=a_recv.at[i], device_id=device, device_id_type=MESH)

    up_far = a_copy(0, 0, 2, 0, HALF, at_y(1, 0))
    down_far = a_copy(1, 0, 6, HALF, SP - HALF, at_y(3, 0))
    up_near = a_copy(2, 0, 2, HALF, SP - HALF, at_y(1, 0))
    down_near = a_copy(3, 0, 6, 0, HALF, at_y(3, 0))
    side = a_copy(4, 0, 1, 0, SP, at_y(0, 1))
    a_copies = [up_far, down_far, up_near, down_near]
    for copy in a_copies:
        copy.start()

    pl.semaphore_wait(met.at[0], 2)
    call_z(1)
    g_load.wait()
    g_pad[0:192, :] = g_raw[0:192, :]
    g_pad[192:SP, :] = jnp.zeros((SP - 192, FF), jnp.bfloat16)
    g_pad[192:S, :] = g_raw[192:S, :]
    own_block = pl.ds(pl.multiple_of(aug * BW, BW), BW)
    own_copy = pltpu.make_async_copy(g_pad.at[:, own_block], g_all.at[pl.ds(0, SP)], own_sem)
    own_copy.start()

    up_far.wait_recv()
    far_up = a_copy(5, 2, 4, 0, HALF, at_y(1, 0))
    far_up.start()
    down_far.wait_recv()
    far_down = a_copy(6, 6, 4, HALF, SP - HALF, at_y(3, 0))
    far_down.start()

    g_copies = [[] for _ in range(CH)]

    def start_g(k, peers):
        for dy, dc in peers:
            i = len(g_copies[k])
            to = lax.rem(y + dy, NY) * 2 + lax.rem(c + dc, 2)
            copy = pltpu.make_async_remote_copy(
                src_ref=g_pad.at[:, pl.ds(pl.multiple_of(to * BW + k * CW, CW), CW)],
                dst_ref=g_all.at[pl.ds((dy * 2 + dc) * SP, SP), pl.ds(k * CW, CW)],
                send_sem=g_send.at[k, i], recv_sem=g_recv.at[k, i], device_id=at_y(dy, dc), device_id_type=MESH)
            copy.start()
            g_copies[k].append(copy)

    side.start()
    start_g(0, same_core + other_core)
    start_g(1, same_core + other_core)
    start_g(2, same_core + other_core)

    pl.semaphore_wait(met.at[1], 2)
    call_z(2)

    def permute(s):
        rows = slice(s * SP, (s + 1) * SP)
        a_perm[rows, :] = jnp.dot(a_all[rows, :], perm[...], preferred_element_type=jnp.float32).astype(jnp.bfloat16)

    up_near.wait_recv()
    side_up = a_copy(7, 2, 3, 0, SP, at_y(0, 1))
    side_up.start()
    down_near.wait_recv()
    side_down = a_copy(8, 6, 7, 0, SP, at_y(0, 1))
    side_down.start()
    permute(0)
    side.wait_recv()
    permute(1)
    permute(2)
    permute(6)
    far_up.wait_recv()
    far_down.wait_recv()
    side_far = a_copy(9, 4, 5, 0, SP, at_y(0, 1))
    side_far.start()
    permute(4)
    side_up.wait_recv()
    permute(3)
    side_down.wait_recv()
    permute(7)
    side_far.wait_recv()
    permute(5)
    a_copies += [side, far_up, far_down, side_up, side_down, side_far]
    own_copy.wait()

    def scale_of(level):
        return jnp.exp2(level.astype(jnp.float32) * (1.0 / 64.0))

    def pack(piece):
        half = piece.shape[0] // 2
        top = jnp.maximum(jnp.max(jnp.abs(piece), axis=0, keepdims=True), 1e-30)
        level = jnp.ceil(jnp.log2(top) * 64.0).astype(jnp.int32) + 1
        ints = jnp.round(piece * (LEVELS / scale_of(level))).astype(jnp.int32)
        return ints[:half] * 65536 + ints[half:], level

    def unpack(words, level, weight):
        high = (words + 32768) >> 16
        low = words - high * 65536
        scale = scale_of(level) * (weight * (1.0 / LEVELS))
        return high.astype(jnp.float32) * scale, low.astype(jnp.float32) * scale

    x_copies = [[] for _ in range(CH)]
    total = jnp.zeros((1, CW), jnp.float32)
    for k in range(CH):
        for copy in g_copies[k]:
            copy.wait_recv()
        cols = slice(k * CW, (k + 1) * CW)
        for h in range(2):
            block = lax.dot_general(
                a_perm[:, h * 2 * XR:(h + 1) * 2 * XR], g_all[:, cols], (((0,), (0,)), ((), ())),
                preferred_element_type=jnp.float32)
            total = total + jnp.sum(block * block, axis=0, keepdims=True)
            if h == 1:
                own_part[:, cols] = block[XR:]
            for t in range(2 - h):
                words, level = pack(block[t * XR:(t + 1) * XR])
                n = h * 2 + t
                x_out[k, n, 0:XR // 2, :] = words
                x_out[k, n, XR // 2:, :] = jnp.broadcast_to(level, (8, CW))
                copy = pltpu.make_async_remote_copy(
                    src_ref=x_out.at[k, n], dst_ref=x_in.at[k, n],
                    send_sem=x_send.at[k, n], recv_sem=x_recv.at[k, n], device_id=at_x(X_ORDER[n]), device_id_type=MESH)
                copy.start()
                x_copies[k].append(copy)

    pl.semaphore_wait(met.at[2], 2)

    square = jnp.sum(total, axis=1, keepdims=True)
    row = lax.broadcasted_iota(jnp.int32, (8, 128), 0)
    stat = jnp.where(row < 4, jnp.broadcast_to(square, (8, 128)), jnp.broadcast_to(mask, (8, 128)))
    stat_out[...] = stat
    s_copies = []
    for i, (dy, dc) in enumerate(aug_peers):
        copy = pltpu.make_async_remote_copy(
            src_ref=stat_out, dst_ref=stat_in.at[i], send_sem=s_send.at[i], recv_sem=s_recv.at[i],
            device_id=at_y(dy, dc), device_id_type=MESH)
        copy.start()
        s_copies.append(copy)
    for copy in s_copies:
        copy.wait_recv()
    near = (stat + stat_in[0]) + (stat_in[3] + stat_in[4])
    far = (stat_in[1] + stat_in[2]) + (stat_in[5] + stat_in[6])
    stat = near + far
    count = stat[4:5, :]
    norm = jnp.sqrt(stat[0:1, :]) / count
    factor = CLIP / jnp.maximum(norm, CLIP)
    weight = factor / count
    norm_ref[...] = norm[:, 0:1]
    fac_out[...] = jnp.broadcast_to(weight, (8, 128))
    f_copies = []
    for n in range(NX - 1):
        copy = pltpu.make_async_remote_copy(
            src_ref=fac_out, dst_ref=fac_in.at[n], send_sem=f_send.at[n], recv_sem=f_recv.at[n],
            device_id=at_x(X_ORDER[n]), device_id_type=MESH)
        copy.start()
        f_copies.append(copy)

    for copy in f_copies:
        copy.wait_recv()
    half = XR // 2
    for k in range(CH):
        cols = slice(k * CW, (k + 1) * CW)
        high, low = weight * own_part[0:half, cols], weight * own_part[half:, cols]
        for n in range(NX - 1):
            x_copies[k][n].wait_recv()
            one, two = unpack(x_in[k, n, 0:half, :], x_in[k, n, half:half + 1, :], fac_in[n, 0:1, :])
            high = high + one
            low = low + two
        parts[0:half, cols] = high
        parts[half:, cols] = low

    z_copies = []
    for d in Z_ORDER:
        words, level = pack(parts[d * ZR:(d + 1) * ZR, :])
        if d == 0:
            own_ref[0:6, :], own_ref[6:12, :] = unpack(words, level, 1.0)
            continue
        z_out[d - 1, 0:6, :] = words
        z_out[d - 1, 6:8, :] = jnp.broadcast_to(level, (2, BW))
        copy = pltpu.make_async_remote_copy(
            src_ref=z_out.at[d - 1], dst_ref=z_in.at[d - 1], send_sem=z_send.at[d - 1], recv_sem=z_recv.at[d - 1],
            device_id=at_z(d), device_id_type=MESH)
        copy.start()
        z_copies.append((d, copy))

    top_rows = low_rows = None
    for d, copy in reversed(z_copies):
        copy.wait_recv()
        words = z_in[d - 1]
        one, two = unpack(words[0:6], words[6:7], 1.0)
        top_rows = one if top_rows is None else top_rows + one
        low_rows = two if low_rows is None else low_rows + two
    rest_ref[0:6, :] = top_rows
    rest_ref[6:12, :] = low_rows

    for copy in a_copies + sum(g_copies, []) + sum(x_copies, []) + s_copies + f_copies + [copy for _, copy in z_copies]:
        copy.wait_send()


def per_device(activations, out_grads, kept_mask, noise_field):
    vmem = pl.BlockSpec(memory_space=pltpu.VMEM)
    hbm = pl.BlockSpec(memory_space=pl.ANY)
    dma = pltpu.SemaphoreType.DMA
    bf16, f32, i32 = jnp.bfloat16, jnp.float32, jnp.int32
    own, rest, norm = pl.pallas_call(
        kernel,
        out_shape=(
            jax.ShapeDtypeStruct((ZR, BW), f32), jax.ShapeDtypeStruct((ZR, BW), f32), jax.ShapeDtypeStruct((1, 1), f32)),
        in_specs=[hbm, hbm, vmem],
        out_specs=(vmem,) * 3,
        scratch_shapes=[
            pltpu.VMEM((S, D), bf16),
            pltpu.VMEM((S, FF), bf16),
            pltpu.VMEM((8 * SP, D), bf16),
            pltpu.VMEM((8 * SP, D), bf16),
            pltpu.VMEM((SP, FF), bf16),
            pltpu.VMEM((8 * SP, BW), bf16),
            pltpu.VMEM((D, D), bf16),
            pltpu.VMEM((XR, BW), f32),
            pltpu.VMEM((CH, NX - 1, XR // 2 + 8, CW), i32),
            pltpu.VMEM((CH, NX - 1, XR // 2 + 8, CW), i32),
            pltpu.VMEM((XR, BW), f32),
            pltpu.VMEM((8, 128), f32),
            pltpu.VMEM((7, 8, 128), f32),
            pltpu.VMEM((8, 128), f32),
            pltpu.VMEM((NX - 1, 8, 128), f32),
            pltpu.VMEM((NZ - 1, 8, BW), i32),
            pltpu.VMEM((NZ - 1, 8, BW), i32),
            dma((2,)), dma((10,)), dma((10,)), dma((CH, 7)), dma((CH, 7)), dma((CH, NX - 1)), dma((CH, NX - 1)),
            dma((7,)), dma((7,)), dma((NX - 1,)), dma((NX - 1,)), dma((NZ - 1,)), dma((NZ - 1,)), dma, pltpu.SemaphoreType.REGULAR((3,)),
        ],
        compiler_params=pltpu.CompilerParams(collective_id=0, has_side_effects=True, vmem_limit_bytes=56 * 2**20),
        name="clipped_sum",
    )(activations[0, 0], out_grads[0, 0], kept_mask)
    clipped = own + rest
    update = (clipped + CLIP * noise_field) * (1.0 / IMAGES)
    return clipped, update, norm.reshape(1)


def solution(mesh):
    in_specs = (
        P("img", "aug", None, None),
        P("img", "aug", None, None),
        P("img", "aug"),
        P("img", "aug"),
    )
    out_specs = (P("img", "aug"), P("img", "aug"), P("img"))
    return jax.shard_map(
        per_device, mesh=mesh, in_specs=in_specs, out_specs=out_specs, check_vma=False
    )
```

time: 68.7 us -> 65.9 us (0.959)
  local copies, waits for them, and re-layouts: 2.69 us -> 0.01 us
  other arithmetic: 0 us -> 1.38 us
  Pallas kernels: 61.6 us -> 60.3 us
    unnamed x2, local copies, waits for them, and re-layouts: 2.69 us -> 0.01 us
    pallas_call x1, Pallas kernels: 61.6 us -> 60.3 us  [per_device(): pl.pallas_call(kernel, out_shape=(jax.ShapeDtypeStruct((ZR, BW), f32), ja...]
    mul x0 -> x1, other arithmetic: none -> 1.38 us  [per_device(): update = (clipped + CLIP * noise_field) * (1.0 / IMAGES)]
where the time goes in v3:
time: 65.9 us; the launch traced here: 64.8 us
  Pallas kernels  60.3 us (92%)
  between operations  3.13 us (5%)
  other arithmetic  1.38 us (2%)
    pallas_call x1, Pallas kernels, per_device(): pl.pallas_call(kernel, out_shape=(jax.ShapeDtypeStruct((ZR, BW), f32), ja...  60.3 us
    mul x1, other arithmetic, per_device(): update = (clipped + CLIP * noise_field) * (1.0 / IMAGES)  1.38 us

profile of v3, /device:TPU:1, one launch (start us, length us, event | category | flops | bytes accessed | tf_op | source)
XLA Modules:
  0.0 64.8 jit_solution(5495212100818047210)
XLA Ops:
  0.6 0.0 copy-start
  1.3 60.3 %clipped_sum.1 = (f32[12,384]{1,0:T(8,128)}, f32[12,384]{1,0:T(8,128)}, f32[1,1]{1,0:T(1,128)}) custom-call(bf16[197,768]{1,0:T(8,128)(2,1)} %bitcast.4, bf16[197,3072]{1,0:T(8,128)(2,1)} %bitcast.3, s32[1,1]{1,0:T(1,128)S(6)} %copy.8.m_ref), custom_call_target="tpu_custom_call" | custom-call | tf_op jit(solution)/shard_map/clipped_sum/pallas_call | solution.py:284
  61.6 0.0 copy-done
  61.6 1.4 %add_multiply_fusion = (f32[12,384]{1,0:T(8,128)}, f32[12,384]{1,0:T(8,128)}) fusion(f32[12,384]{1,0:T(8,128)S(1)} %copy-done, f32[12,384]{1,0:T(8,128)} %get-tuple-element.6, f32[12,384]{1,0:T(8,128)} %get-tuple-element.7), kind=kLoop, calls=%fused_computation | loop fusion | flops 18432 | bytes 92160 | tf_op jit(solution)/shard_map/mul | solution.py:315
Async XLA Ops:
  0.6 60.9 %copy-start = (f32[12,384]{1,0:T(8,128)S(1)}, f32[12,384]{1,0:T(8,128)}, u32[]{:S(2)}) copy-start(f32[12,384]{1,0:T(8,128)} %param.7) | copy-start | bytes 55300

commit v4 on v3

--- a/solution.py
+++ b/solution.py
@@ -15,14 +15,14 @@
 BW = FF // 8
 CH = 3
 CW = BW // CH
-XR = D // NX
+XR = D // 8
 ZR = D // (NX * NZ)
 HALF = 112
 IMAGES = 64
 CLIP = 0.01 * math.sqrt(D * FF * S)
 LEVELS = 32766.0
-X_ORDER = (2, 1, 3, 0)
-Z_ORDER = (8, 7, 9, 6, 10, 5, 11, 4, 12, 3, 13, 2, 14, 1, 15, 0)
+GROUP = ((2, 1), (2, 0), (1, 1), (1, 0), (3, 1), (3, 0), (0, 1), (0, 0))
+Z_ORDER = (4, 3, 5, 2, 6, 1, 7, 0)
 
 
 def kernel(
@@ -38,8 +38,10 @@
     def at_y(dy, dc):
         return (img, lax.rem(y + dy, NY) * 2 + (lax.rem(c + dc, 2)))
 
-    def at_x(dx):
-        return (z * NX + lax.rem(x + dx, NX), aug)
+    pair = z + 1 - 2 * lax.rem(z, 2)
+
+    def in_group(dx, other):
+        return ((pair if other else z) * NX + lax.rem(x + dx, NX), aug)
 
     def at_z(dz):
         return (lax.rem(z + dz + NZ, NZ) * NX + x, aug)
@@ -51,10 +53,9 @@
     barrier = pltpu.get_barrier_semaphore()
     for dy, dc in aug_peers:
         pl.semaphore_signal(barrier, inc=1, device_id=at_y(dy, dc), device_id_type=MESH)
-    for dx in range(1, NX):
-        pl.semaphore_signal(barrier, inc=1, device_id=at_x(dx), device_id_type=MESH)
-    for dz in (1, -1):
-        pl.semaphore_signal(barrier, inc=1, device_id=at_z(dz), device_id_type=MESH)
+    for dx, other in GROUP[:7]:
+        pl.semaphore_signal(barrier, inc=1, device_id=in_group(dx, other), device_id_type=MESH)
+    pl.semaphore_signal(barrier, inc=1, device_id=at_z(1 - 2 * lax.rem(z + 1, 2)), device_id_type=MESH)
 
     a_load = pltpu.make_async_copy(a_hbm, a_raw, in_sem.at[0])
     g_load = pltpu.make_async_copy(g_hbm, g_raw, in_sem.at[1])
@@ -62,9 +63,10 @@
     g_load.start()
 
     p = lax.broadcasted_iota(jnp.int32, (1, D), 1)
-    px, pz, pr = p // XR, lax.rem(p, XR) // ZR, lax.rem(p, ZR)
-    to_x = lax.rem(x + jnp.where(px == 0, 2, jnp.where(px == 3, 0, px * 2 - 1)), NX)
-    source = lax.rem(z + pz, NZ) * (NX * ZR) + to_x * ZR + pr
+    pn, pj, pr = p // XR, lax.rem(p, XR) // ZR, lax.rem(p, ZR)
+    step_x = jnp.where(pn < 2, 2, jnp.where(pn < 4, 1, jnp.where(pn < 6, 3, 0)))
+    from_z = jnp.where(lax.rem(pn, 2) == 0, pair, z)
+    source = lax.rem(from_z + 2 * pj, NZ) * (NX * ZR) + lax.rem(x + step_x, NX) * ZR + pr
     perm[...] = (lax.broadcasted_iota(jnp.int32, (D, D), 0) == source).astype(jnp.bfloat16)
 
     mask = m_ref[...].astype(jnp.float32)
@@ -73,7 +75,7 @@
     a_all[192:SP, :] = jnp.zeros((SP - 192, D), jnp.bfloat16)
     a_all[192:S, :] = (a_raw[192:S, :].astype(jnp.float32) * mask).astype(jnp.bfloat16)
 
-    pl.semaphore_wait(barrier, 7 + (NX - 1) + 2)
+    pl.semaphore_wait(barrier, 7 + 7 + 1)
 
     def call_z(step):
         for dz in (1 << step, -(1 << step)):
@@ -186,19 +188,19 @@
         cols = slice(k * CW, (k + 1) * CW)
         for h in range(2):
             block = lax.dot_general(
-                a_perm[:, h * 2 * XR:(h + 1) * 2 * XR], g_all[:, cols], (((0,), (0,)), ((), ())),
+                a_perm[:, h * 4 * XR:(h + 1) * 4 * XR], g_all[:, cols], (((0,), (0,)), ((), ())),
                 preferred_element_type=jnp.float32)
             total = total + jnp.sum(block * block, axis=0, keepdims=True)
             if h == 1:
-                own_part[:, cols] = block[XR:]
-            for t in range(2 - h):
+                own_part[:, cols] = block[3 * XR:]
+            for t in range(4 - h):
                 words, level = pack(block[t * XR:(t + 1) * XR])
-                n = h * 2 + t
+                n = h * 4 + t
                 x_out[k, n, 0:XR // 2, :] = words
                 x_out[k, n, XR // 2:, :] = jnp.broadcast_to(level, (8, CW))
                 copy = pltpu.make_async_remote_copy(
                     src_ref=x_out.at[k, n], dst_ref=x_in.at[k, n],
-                    send_sem=x_send.at[k, n], recv_sem=x_recv.at[k, n], device_id=at_x(X_ORDER[n]), device_id_type=MESH)
+                    send_sem=x_send.at[k, n], recv_sem=x_recv.at[k, n], device_id=in_group(*GROUP[n]), device_id_type=MESH)
                 copy.start()
                 x_copies[k].append(copy)
 
@@ -227,10 +229,10 @@
     norm_ref[...] = norm[:, 0:1]
     fac_out[...] = jnp.broadcast_to(weight, (8, 128))
     f_copies = []
-    for n in range(NX - 1):
+    for n in range(7):
         copy = pltpu.make_async_remote_copy(
             src_ref=fac_out, dst_ref=fac_in.at[n], send_sem=f_send.at[n], recv_sem=f_recv.at[n],
-            device_id=at_x(X_ORDER[n]), device_id_type=MESH)
+            device_id=in_group(*GROUP[n]), device_id_type=MESH)
         copy.start()
         f_copies.append(copy)
 
@@ -240,7 +242,7 @@
     for k in range(CH):
         cols = slice(k * CW, (k + 1) * CW)
         high, low = weight * own_part[0:half, cols], weight * own_part[half:, cols]
-        for n in range(NX - 1):
+        for n in range(7):
             x_copies[k][n].wait_recv()
             one, two = unpack(x_in[k, n, 0:half, :], x_in[k, n, half:half + 1, :], fac_in[n, 0:1, :])
             high = high + one
@@ -258,7 +260,7 @@
         z_out[d - 1, 6:8, :] = jnp.broadcast_to(level, (2, BW))
         copy = pltpu.make_async_remote_copy(
             src_ref=z_out.at[d - 1], dst_ref=z_in.at[d - 1], send_sem=z_send.at[d - 1], recv_sem=z_recv.at[d - 1],
-            device_id=at_z(d), device_id_type=MESH)
+            device_id=at_z(2 * d), device_id_type=MESH)
         copy.start()
         z_copies.append((d, copy))
 
@@ -296,17 +298,17 @@
             pltpu.VMEM((8 * SP, BW), bf16),
             pltpu.VMEM((D, D), bf16),
             pltpu.VMEM((XR, BW), f32),
-            pltpu.VMEM((CH, NX - 1, XR // 2 + 8, CW), i32),
-            pltpu.VMEM((CH, NX - 1, XR // 2 + 8, CW), i32),
+            pltpu.VMEM((CH, 7, XR // 2 + 8, CW), i32),
+            pltpu.VMEM((CH, 7, XR // 2 + 8, CW), i32),
             pltpu.VMEM((XR, BW), f32),
             pltpu.VMEM((8, 128), f32),
             pltpu.VMEM((7, 8, 128), f32),
             pltpu.VMEM((8, 128), f32),
-            pltpu.VMEM((NX - 1, 8, 128), f32),
-            pltpu.VMEM((NZ - 1, 8, BW), i32),
-            pltpu.VMEM((NZ - 1, 8, BW), i32),
-            dma((2,)), dma((10,)), dma((10,)), dma((CH, 7)), dma((CH, 7)), dma((CH, NX - 1)), dma((CH, NX - 1)),
-            dma((7,)), dma((7,)), dma((NX - 1,)), dma((NX - 1,)), dma((NZ - 1,)), dma((NZ - 1,)), dma, pltpu.SemaphoreType.REGULAR((3,)),
+            pltpu.VMEM((7, 8, 128), f32),
+            pltpu.VMEM((7, 8, BW), i32),
+            pltpu.VMEM((7, 8, BW), i32),
+            dma((2,)), dma((10,)), dma((10,)), dma((CH, 7)), dma((CH, 7)), dma((CH, 7)), dma((CH, 7)),
+            dma((7,)), dma((7,)), dma((7,)), dma((7,)), dma((7,)), dma((7,)), dma, pltpu.SemaphoreType.REGULAR((3,)),
         ],
         compiler_params=pltpu.CompilerParams(collective_id=0, has_side_effects=True, vmem_limit_bytes=56 * 2**20),
         name="clipped_sum",

time: 65.9 us -> 63.6 us (0.965); the launches traced: 64.8 us -> 63.2 us
  Pallas kernels: 60.3 us -> 58.7 us
    pallas_call x1, Pallas kernels: 60.3 us -> 58.7 us  [per_device(): pl.pallas_call(kernel, out_shape=(jax.ShapeDtypeStruct((ZR, BW), f32), ja...]
where the time goes in v4:
time: 63.6 us; the launch traced here: 63.2 us
  Pallas kernels  58.7 us (92%)
  between operations  3.13 us (5%)
  other arithmetic  1.38 us (2%)
    pallas_call x1, Pallas kernels, per_device(): pl.pallas_call(kernel, out_shape=(jax.ShapeDtypeStruct((ZR, BW), f32), ja...  58.7 us
    mul x1, other arithmetic, per_device(): update = (clipped + CLIP * noise_field) * (1.0 / IMAGES)  1.38 us

profile of v4, /device:TPU:1, one launch (start us, length us, event | category | flops | bytes accessed | tf_op | source)
XLA Modules:
  0.0 63.2 jit_solution(6844164162242787652)
XLA Ops:
  0.6 0.0 copy-start
  1.3 58.7 %clipped_sum.1 = (f32[12,384]{1,0:T(8,128)}, f32[12,384]{1,0:T(8,128)}, f32[1,1]{1,0:T(1,128)}) custom-call(bf16[197,768]{1,0:T(8,128)(2,1)} %bitcast.4, bf16[197,3072]{1,0:T(8,128)(2,1)} %bitcast.3, s32[1,1]{1,0:T(1,128)S(6)} %copy.8.m_ref), custom_call_target="tpu_custom_call" | custom-call | tf_op jit(solution)/shard_map/clipped_sum/pallas_call | solution.py:286
  60.0 0.0 copy-done
  60.0 1.4 %add_multiply_fusion = (f32[12,384]{1,0:T(8,128)}, f32[12,384]{1,0:T(8,128)}) fusion(f32[12,384]{1,0:T(8,128)S(1)} %copy-done, f32[12,384]{1,0:T(8,128)} %get-tuple-element.6, f32[12,384]{1,0:T(8,128)} %get-tuple-element.7), kind=kLoop, calls=%fused_computation | loop fusion | flops 18432 | bytes 92160 | tf_op jit(solution)/shard_map/mul | solution.py:317
Async XLA Ops:
  0.6 59.4 %copy-start = (f32[12,384]{1,0:T(8,128)S(1)}, f32[12,384]{1,0:T(8,128)}, u32[]{:S(2)}) copy-start(f32[12,384]{1,0:T(8,128)} %param.7) | copy-start | bytes 55300

commit v5 on v4

--- a/solution.py
+++ b/solution.py
@@ -17,7 +17,6 @@
 CW = BW // CH
 XR = D // 8
 ZR = D // (NX * NZ)
-HALF = 112
 IMAGES = 64
 CLIP = 0.01 * math.sqrt(D * FF * S)
 LEVELS = 32766.0
@@ -28,15 +27,20 @@
 def kernel(
     a_hbm, g_hbm, m_ref,
     own_ref, rest_ref, norm_ref,
-    a_raw, g_raw, a_all, a_perm, g_pad, g_all, perm, own_part, x_out, x_in, parts,
+    a_raw, g_raw, a_all, a_perm, g_pad, g_all, perm, half_sum, p_out, p_in, own_part, x_out, x_in, parts,
     stat_out, stat_in, fac_out, fac_in, z_out, z_in,
-    in_sem, a_send, a_recv, g_send, g_recv, x_send, x_recv, s_send, s_recv, f_send, f_recv, z_send, z_recv, own_sem, met,
+    in_sem, a_send, a_recv, g_send, g_recv, p_send, p_recv, x_send, x_recv, s_send, s_recv, f_send, f_recv, z_send, z_recv, own_sem, met,
 ):
     img, aug = lax.axis_index("img"), lax.axis_index("aug")
     z, x, y, c = img // NX, lax.rem(img, NX), aug // 2, lax.rem(aug, 2)
 
+    mate = (1 - 2 * lax.rem(y, 2)) * (1 - 2 * c)
+
     def at_y(dy, dc):
-        return (img, lax.rem(y + dy, NY) * 2 + (lax.rem(c + dc, 2)))
+        return (img, lax.rem(y + dy + NY, NY) * 2 + (lax.rem(c + dc, 2)))
+
+    def block_of(dy, dc):
+        return lax.rem(y + dy + NY, NY) * 2 + lax.rem(c + dc, 2)
 
     pair = z + 1 - 2 * lax.rem(z, 2)
 
@@ -46,8 +50,11 @@
     def at_z(dz):
         return (lax.rem(z + dz + NZ, NZ) * NX + x, aug)
 
-    same_core = [(1, 0), (3, 0), (2, 0)]
-    other_core = [(0, 1), (1, 1), (3, 1), (2, 1)]
+    partners = (
+        (2, (mate, 0), ((2, 0), (mate, 0))),
+        (3, (-mate, 1), ((2, 1), (-mate, 1))),
+        (1, (0, 1), ((mate, 1), (0, 1))),
+    )
     aug_peers = [(dy, dc) for dy in range(NY) for dc in range(2) if (dy, dc) != (0, 0)]
 
     barrier = pltpu.get_barrier_semaphore()
@@ -62,6 +69,58 @@
     a_load.start()
     g_load.start()
 
+    mask = m_ref[...].astype(jnp.float32)
+    a_load.wait()
+    a_all[0:192, :] = (a_raw[0:192, :].astype(jnp.float32) * mask).astype(jnp.bfloat16)
+    a_all[192:SP, :] = jnp.zeros((SP - 192, D), jnp.bfloat16)
+    a_all[192:S, :] = (a_raw[192:S, :].astype(jnp.float32) * mask).astype(jnp.bfloat16)
+
+    pl.semaphore_wait(barrier, 7 + 7 + 1)
+
+    def call_z(step):
+        for dz in (1 << step, -(1 << step)):
+            pl.semaphore_signal(met.at[step], inc=1, device_id=at_z(dz), device_id_type=MESH)
+
+    call_z(0)
+
+    a_copies = []
+    for slot, device, _ in partners:
+        copy = pltpu.make_async_remote_copy(
+            src_ref=a_all.at[pl.ds(0, SP)], dst_ref=a_all.at[pl.ds(slot * SP, SP)],
+            send_sem=a_send.at[slot - 1], recv_sem=a_recv.at[slot - 1], device_id=at_y(*device), device_id_type=MESH)
+        copy.start()
+        a_copies.append(copy)
+
+    pl.semaphore_wait(met.at[0], 2)
+    call_z(1)
+    g_load.wait()
+    g_pad[0:192, :] = g_raw[0:192, :]
+    g_pad[192:SP, :] = jnp.zeros((SP - 192, FF), jnp.bfloat16)
+    g_pad[192:S, :] = g_raw[192:S, :]
+    def columns(block, k, width):
+        return pl.ds(pl.multiple_of(block * BW + k * CW, CW), width)
+
+    own_copies = []
+    for b, block in enumerate((block_of(-mate, 0), block_of(0, 0))):
+        copy = pltpu.make_async_copy(g_pad.at[:, columns(block, 0, BW)], g_all.at[b, pl.ds(0, SP)], own_sem.at[b])
+        copy.start()
+        own_copies.append(copy)
+    g_copies = {}
+    for b in range(2):
+        for k in range(CH):
+            g_copies[b, k] = []
+            for slot, device, blocks in partners:
+                copy = pltpu.make_async_remote_copy(
+                    src_ref=g_pad.at[:, columns(block_of(*blocks[b]), k, CW)],
+                    dst_ref=g_all.at[b, pl.ds(slot * SP, SP), pl.ds(k * CW, CW)],
+                    send_sem=g_send.at[b, k, slot - 1], recv_sem=g_recv.at[b, k, slot - 1],
+                    device_id=at_y(*device), device_id_type=MESH)
+                copy.start()
+                g_copies[b, k].append(copy)
+
+    pl.semaphore_wait(met.at[1], 2)
+    call_z(2)
+
     p = lax.broadcasted_iota(jnp.int32, (1, D), 1)
     pn, pj, pr = p // XR, lax.rem(p, XR) // ZR, lax.rem(p, ZR)
     step_x = jnp.where(pn < 2, 2, jnp.where(pn < 4, 1, jnp.where(pn < 6, 3, 0)))
@@ -69,100 +128,16 @@
     source = lax.rem(from_z + 2 * pj, NZ) * (NX * ZR) + lax.rem(x + step_x, NX) * ZR + pr
     perm[...] = (lax.broadcasted_iota(jnp.int32, (D, D), 0) == source).astype(jnp.bfloat16)
 
-    mask = m_ref[...].astype(jnp.float32)
-    a_load.wait()
-    a_all[0:192, :] = (a_raw[0:192, :].astype(jnp.float32) * mask).astype(jnp.bfloat16)
-    a_all[192:SP, :] = jnp.zeros((SP - 192, D), jnp.bfloat16)
-    a_all[192:S, :] = (a_raw[192:S, :].astype(jnp.float32) * mask).astype(jnp.bfloat16)
-
-    pl.semaphore_wait(barrier, 7 + 7 + 1)
-
-    def call_z(step):
-        for dz in (1 << step, -(1 << step)):
-            pl.semaphore_signal(met.at[step], inc=1, device_id=at_z(dz), device_id_type=MESH)
-
-    call_z(0)
-
-    def a_copy(i, src, dst, first, rows, device):
-        return pltpu.make_async_remote_copy(
-            src_ref=a_all.at[pl.ds(src * SP + first, rows)], dst_ref=a_all.at[pl.ds(dst * SP + first, rows)],
-            send_sem=a_send.at[i], recv_sem=a_recv.at[i], device_id=device, device_id_type=MESH)
-
-    up_far = a_copy(0, 0, 2, 0, HALF, at_y(1, 0))
-    down_far = a_copy(1, 0, 6, HALF, SP - HALF, at_y(3, 0))
-    up_near = a_copy(2, 0, 2, HALF, SP - HALF, at_y(1, 0))
-    down_near = a_copy(3, 0, 6, 0, HALF, at_y(3, 0))
-    side = a_copy(4, 0, 1, 0, SP, at_y(0, 1))
-    a_copies = [up_far, down_far, up_near, down_near]
-    for copy in a_copies:
-        copy.start()
-
-    pl.semaphore_wait(met.at[0], 2)
-    call_z(1)
-    g_load.wait()
-    g_pad[0:192, :] = g_raw[0:192, :]
-    g_pad[192:SP, :] = jnp.zeros((SP - 192, FF), jnp.bfloat16)
-    g_pad[192:S, :] = g_raw[192:S, :]
-    own_block = pl.ds(pl.multiple_of(aug * BW, BW), BW)
-    own_copy = pltpu.make_async_copy(g_pad.at[:, own_block], g_all.at[pl.ds(0, SP)], own_sem)
-    own_copy.start()
-
-    up_far.wait_recv()
-    far_up = a_copy(5, 2, 4, 0, HALF, at_y(1, 0))
-    far_up.start()
-    down_far.wait_recv()
-    far_down = a_copy(6, 6, 4, HALF, SP - HALF, at_y(3, 0))
-    far_down.start()
-
-    g_copies = [[] for _ in range(CH)]
-
-    def start_g(k, peers):
-        for dy, dc in peers:
-            i = len(g_copies[k])
-            to = lax.rem(y + dy, NY) * 2 + lax.rem(c + dc, 2)
-            copy = pltpu.make_async_remote_copy(
-                src_ref=g_pad.at[:, pl.ds(pl.multiple_of(to * BW + k * CW, CW), CW)],
-                dst_ref=g_all.at[pl.ds((dy * 2 + dc) * SP, SP), pl.ds(k * CW, CW)],
-                send_sem=g_send.at[k, i], recv_sem=g_recv.at[k, i], device_id=at_y(dy, dc), device_id_type=MESH)
-            copy.start()
-            g_copies[k].append(copy)
-
-    side.start()
-    start_g(0, same_core + other_core)
-    start_g(1, same_core + other_core)
-    start_g(2, same_core + other_core)
-
-    pl.semaphore_wait(met.at[1], 2)
-    call_z(2)
-
     def permute(s):
         rows = slice(s * SP, (s + 1) * SP)
         a_perm[rows, :] = jnp.dot(a_all[rows, :], perm[...], preferred_element_type=jnp.float32).astype(jnp.bfloat16)
 
-    up_near.wait_recv()
-    side_up = a_copy(7, 2, 3, 0, SP, at_y(0, 1))
-    side_up.start()
-    down_near.wait_recv()
-    side_down = a_copy(8, 6, 7, 0, SP, at_y(0, 1))
-    side_down.start()
     permute(0)
-    side.wait_recv()
-    permute(1)
-    permute(2)
-    permute(6)
-    far_up.wait_recv()
-    far_down.wait_recv()
-    side_far = a_copy(9, 4, 5, 0, SP, at_y(0, 1))
-    side_far.start()
-    permute(4)
-    side_up.wait_recv()
-    permute(3)
-    side_down.wait_recv()
-    permute(7)
-    side_far.wait_recv()
-    permute(5)
-    a_copies += [side, far_up, far_down, side_up, side_down, side_far]
-    own_copy.wait()
+    for copy, slot in zip(reversed(a_copies), (1, 3, 2)):
+        copy.wait_recv()
+        permute(slot)
+    for copy in own_copies:
+        copy.wait()
 
     def scale_of(level):
         return jnp.exp2(level.astype(jnp.float32) * (1.0 / 64.0))
@@ -180,16 +155,39 @@
         scale = scale_of(level) * (weight * (1.0 / LEVELS))
         return high.astype(jnp.float32) * scale, low.astype(jnp.float32) * scale
 
+    half = D // 2
+    p_copies = {}
+    for b in range(2):
+        for k in range(CH):
+            for copy in g_copies[b, k]:
+                copy.wait_recv()
+            cols = slice(k * CW, (k + 1) * CW)
+            for h in range(2):
+                block = lax.dot_general(
+                    a_perm[:, h * half:(h + 1) * half], g_all[b, :, cols], (((0,), (0,)), ((), ())),
+                    preferred_element_type=jnp.float32)
+                if b:
+                    half_sum[h * half:(h + 1) * half, cols] = block
+                    continue
+                words, level = pack(block)
+                p_out[k, h, 0:half // 2, :] = words
+                p_out[k, h, half // 2:, :] = jnp.broadcast_to(level, (8, CW))
+                copy = pltpu.make_async_remote_copy(
+                    src_ref=p_out.at[k, h], dst_ref=p_in.at[k, h],
+                    send_sem=p_send.at[k, h], recv_sem=p_recv.at[k, h], device_id=at_y(-mate, 0), device_id_type=MESH)
+                copy.start()
+                p_copies[k, h] = copy
+    for copy in a_copies + sum(g_copies.values(), []):
+        copy.wait_send()
+
     x_copies = [[] for _ in range(CH)]
     total = jnp.zeros((1, CW), jnp.float32)
     for k in range(CH):
-        for copy in g_copies[k]:
-            copy.wait_recv()
         cols = slice(k * CW, (k + 1) * CW)
         for h in range(2):
-            block = lax.dot_general(
-                a_perm[:, h * 4 * XR:(h + 1) * 4 * XR], g_all[:, cols], (((0,), (0,)), ((), ())),
-                preferred_element_type=jnp.float32)
+            p_copies[k, h].wait_recv()
+            parts_of = unpack(p_in[k, h, 0:half // 2, :], p_in[k, h, half // 2:half // 2 + 1, :], 1.0)
+            block = jnp.concatenate(parts_of, axis=0) + half_sum[h * half:(h + 1) * half, cols]
             total = total + jnp.sum(block * block, axis=0, keepdims=True)
             if h == 1:
                 own_part[:, cols] = block[3 * XR:]
@@ -264,6 +262,8 @@
         copy.start()
         z_copies.append((d, copy))
 
+    for copy in list(p_copies.values()) + sum(x_copies, []) + s_copies + f_copies:
+        copy.wait_send()
     top_rows = low_rows = None
     for d, copy in reversed(z_copies):
         copy.wait_recv()
@@ -274,7 +274,7 @@
     rest_ref[0:6, :] = top_rows
     rest_ref[6:12, :] = low_rows
 
-    for copy in a_copies + sum(g_copies, []) + sum(x_copies, []) + s_copies + f_copies + [copy for _, copy in z_copies]:
+    for _, copy in z_copies:
         copy.wait_send()
 
 
@@ -292,11 +292,14 @@
         scratch_shapes=[
             pltpu.VMEM((S, D), bf16),
             pltpu.VMEM((S, FF), bf16),
-            pltpu.VMEM((8 * SP, D), bf16),
-            pltpu.VMEM((8 * SP, D), bf16),
+            pltpu.VMEM((4 * SP, D), bf16),
+            pltpu.VMEM((4 * SP, D), bf16),
             pltpu.VMEM((SP, FF), bf16),
-            pltpu.VMEM((8 * SP, BW), bf16),
+            pltpu.VMEM((2, 4 * SP, BW), bf16),
             pltpu.VMEM((D, D), bf16),
+            pltpu.VMEM((D, BW), f32),
+            pltpu.VMEM((CH, 2, D // 4 + 8, CW), i32),
+            pltpu.VMEM((CH, 2, D // 4 + 8, CW), i32),
             pltpu.VMEM((XR, BW), f32),
             pltpu.VMEM((CH, 7, XR // 2 + 8, CW), i32),
             pltpu.VMEM((CH, 7, XR // 2 + 8, CW), i32),
@@ -307,10 +310,10 @@
             pltpu.VMEM((7, 8, 128), f32),
             pltpu.VMEM((7, 8, BW), i32),
             pltpu.VMEM((7, 8, BW), i32),
-            dma((2,)), dma((10,)), dma((10,)), dma((CH, 7)), dma((CH, 7)), dma((CH, 7)), dma((CH, 7)),
-            dma((7,)), dma((7,)), dma((7,)), dma((7,)), dma((7,)), dma((7,)), dma, pltpu.SemaphoreType.REGULAR((3,)),
+            dma((2,)), dma((3,)), dma((3,)), dma((2, CH, 3)), dma((2, CH, 3)), dma((CH, 2)), dma((CH, 2)), dma((CH, 7)), dma((CH, 7)),
+            dma((7,)), dma((7,)), dma((7,)), dma((7,)), dma((7,)), dma((7,)), dma((2,)), pltpu.SemaphoreType.REGULAR((3,)),
         ],
-        compiler_params=pltpu.CompilerParams(collective_id=0, has_side_effects=True, vmem_limit_bytes=56 * 2**20),
+        compiler_params=pltpu.CompilerParams(collective_id=0, has_side_effects=True, vmem_limit_bytes=53 * 2**20 + 700000),
         name="clipped_sum",
     )(activations[0, 0], out_grads[0, 0], kept_mask)
     clipped = own + rest

time: 63.6 us -> 57.2 us (0.90)
  Pallas kernels: 58.7 us -> 53.3 us
  other arithmetic: 1.38 us -> 0.62 us
    pallas_call x1, Pallas kernels: 58.7 us -> 53.3 us  [per_device(): pl.pallas_call(kernel, out_shape=(jax.ShapeDtypeStruct((ZR, BW), f32), ja...]
    mul x1, other arithmetic: 1.38 us -> 0.62 us  [per_device(): update = (clipped + CLIP * noise_field) * (1.0 / IMAGES)]
where the time goes in v5:
time: 57.2 us; the launch traced here: 57 us
  Pallas kernels  53.3 us (93%)
  between operations  3.07 us (5%)
  other arithmetic  0.62 us (1%)
    pallas_call x1, Pallas kernels, per_device(): pl.pallas_call(kernel, out_shape=(jax.ShapeDtypeStruct((ZR, BW), f32), ja...  53.3 us

profile of v5, /device:TPU:1, one launch (start us, length us, event | category | flops | bytes accessed | tf_op | source)
XLA Modules:
  0.0 57.0 jit_solution(15727755657283936138)
XLA Ops:
  0.6 0.0 copy-start
  1.3 53.3 %clipped_sum.1 = (f32[12,384]{1,0:T(8,128)S(1)}, f32[12,384]{1,0:T(8,128)S(1)}, f32[1,1]{1,0:T(1,128)}) custom-call(bf16[197,768]{1,0:T(8,128)(2,1)} %bitcast.4, bf16[197,3072]{1,0:T(8,128)(2,1)} %bitcast.3, s32[1,1]{1,0:T(1,128)S(6)} %copy.8.m_ref), custom_call_target="tpu_custom_call" | custom-call | tf_op jit(solution)/shard_map/clipped_sum/pallas_call | solution.py:286
  54.6 0.0 copy-done
  54.6 0.6 %add_multiply_fusion = (f32[12,384]{1,0:T(8,128)}, f32[12,384]{1,0:T(8,128)}) fusion(f32[12,384]{1,0:T(8,128)S(1)} %copy-done, f32[12,384]{1,0:T(8,128)S(1)} %get-tuple-element.6, f32[12,384]{1,0:T(8,128)S(1)} %get-tuple-element.7), kind=kLoop, calls=%fused_computation | loop fusion | flops 18432 | bytes 92160 | tf_op jit(solution)/shard_map/mul | solution.py:320
Async XLA Ops:
  0.6 54.0 %copy-start = (f32[12,384]{1,0:T(8,128)S(1)}, f32[12,384]{1,0:T(8,128)}, u32[]{:S(2)}) copy-start(f32[12,384]{1,0:T(8,128)} %param.7) | copy-start | bytes 55300

commit v6 on v5

v6 whole, which is shorter than its diff:
```python
import functools
import math

import jax
import jax.numpy as jnp
from jax import lax
from jax.experimental import pallas as pl
from jax.experimental.pallas import tpu as pltpu
from jax.sharding import PartitionSpec as P

MESH = pl.DeviceIdType.MESH
NZ, NX, NY = 16, 4, 4
S, D, FF = 197, 768, 3072
SP = 208
BW = FF // 8
CH = 3
CW = BW // CH
XR = D // 8
ZR = D // (NX * NZ)
IMAGES = 64
CLIP = 0.01 * math.sqrt(D * FF * S)
LEVELS = 32766.0
GROUP = ((2, 1), (2, 0), (1, 1), (1, 0), (3, 1), (3, 0), (0, 1), (0, 0))
Z_ORDER = (4, 3, 5, 2, 6, 1, 7, 0)


def kernel(
    a_hbm, g_hbm, m_ref,
    own_ref, rest_ref, norm_ref,
    a_raw, g_raw, a_all, a_perm, g_pad, g_all, perm, half_sum, p_out, p_in, own_part, x_out, x_in, x_part, parts,
    stat_out, stat_in, fac_out, fac_in, z_out, z_in,
    in_sem, a_send, a_recv, g_send, g_recv, p_send, p_recv, x_send, x_recv, s_send, s_recv, f_send, f_recv, z_send, z_recv, own_sem, met,
):
    img, aug = lax.axis_index("img"), lax.axis_index("aug")
    z, x, y, c = img // NX, lax.rem(img, NX), aug // 2, lax.rem(aug, 2)

    mate = (1 - 2 * lax.rem(y, 2)) * (1 - 2 * c)

    def at_y(dy, dc):
        return (img, lax.rem(y + dy + NY, NY) * 2 + (lax.rem(c + dc, 2)))

    def block_of(dy, dc):
        return lax.rem(y + dy + NY, NY) * 2 + lax.rem(c + dc, 2)

    pair = z + 1 - 2 * lax.rem(z, 2)

    def in_group(dx, other):
        return ((pair if other else z) * NX + lax.rem(x + dx, NX), aug)

    def at_z(dz):
        return (lax.rem(z + dz + NZ, NZ) * NX + x, aug)

    partners = (
        (2, (mate, 0), ((2, 0), (mate, 0))),
        (3, (-mate, 1), ((2, 1), (-mate, 1))),
        (1, (0, 1), ((mate, 1), (0, 1))),
    )
    aug_peers = [(dy, dc) for dy in range(NY) for dc in range(2) if (dy, dc) != (0, 0)]

    barrier = pltpu.get_barrier_semaphore()
    next_to = [at_y(0, 1), at_y(1, 0), at_y(1, 1), at_y(-1, 0), at_y(-1, 1)]
    next_to += [in_group(1, 0), in_group(NX - 1, 0), at_z(1), at_z(-1)]
    for device in next_to:
        pl.semaphore_signal(barrier, inc=1, device_id=device, device_id_type=MESH)

    a_load = pltpu.make_async_copy(a_hbm, a_raw, in_sem.at[0])
    g_load = pltpu.make_async_copy(g_hbm, g_raw, in_sem.at[1])
    a_load.start()
    g_load.start()

    mask = m_ref[...].astype(jnp.float32)
    a_load.wait()
    a_all[0:192, :] = (a_raw[0:192, :].astype(jnp.float32) * mask).astype(jnp.bfloat16)
    a_all[192:SP, :] = jnp.zeros((SP - 192, D), jnp.bfloat16)
    a_all[192:S, :] = (a_raw[192:S, :].astype(jnp.float32) * mask).astype(jnp.bfloat16)

    pl.semaphore_wait(barrier, 9)

    def call(step, devices):
        for device in devices:
            pl.semaphore_signal(met.at[step], inc=1, device_id=device, device_id_type=MESH)

    call(0, [at_y(1, 0), in_group(1, 0), in_group(NX - 1, 0), at_z(1), at_z(-1)])

    def whole(ref, sem):
        pltpu.make_async_copy(ref, ref, sem).wait()

    a_copies = []
    for slot, device, _ in partners:
        copy = pltpu.make_async_remote_copy(
            src_ref=a_all.at[pl.ds(0, SP)], dst_ref=a_all.at[pl.ds(slot * SP, SP)],
            send_sem=a_send, recv_sem=a_recv.at[slot - 1], device_id=at_y(*device), device_id_type=MESH)
        copy.start()
        a_copies.append(copy)

    pl.semaphore_wait(met.at[0], 5)
    call(1, [in_group(1, 0), at_z(2), at_z(-2)])
    g_load.wait()
    g_pad[0:192, :] = g_raw[0:192, :]
    g_pad[192:SP, :] = jnp.zeros((SP - 192, FF), jnp.bfloat16)
    g_pad[192:S, :] = g_raw[192:S, :]
    def columns(block, k, width):
        return pl.ds(pl.multiple_of(block * BW + k * CW, CW), width)

    for b, block in enumerate((block_of(-mate, 0), block_of(0, 0))):
        copy = pltpu.make_async_copy(g_pad.at[:, columns(block, 0, BW)], g_all.at[b, pl.ds(0, SP)], own_sem)
        copy.start()
    for b in range(2):
        for k in range(CH):
            for slot, device, blocks in partners:
                copy = pltpu.make_async_remote_copy(
                    src_ref=g_pad.at[:, columns(block_of(*blocks[b]), k, CW)],
                    dst_ref=g_all.at[b, pl.ds(slot * SP, SP), pl.ds(k * CW, CW)],
                    send_sem=g_send, recv_sem=g_recv.at[b, k],
                    device_id=at_y(*device), device_id_type=MESH)
                copy.start()

    pl.semaphore_wait(met.at[1], 3)
    call(2, [at_z(4), at_z(-4)])

    p = lax.broadcasted_iota(jnp.int32, (1, D), 1)
    pn, pj, pr = p // XR, lax.rem(p, XR) // ZR, lax.rem(p, ZR)
    step_x = jnp.where(pn < 2, 2, jnp.where(pn < 4, 1, jnp.where(pn < 6, 3, 0)))
    from_z = jnp.where(lax.rem(pn, 2) == 0, pair, z)
    source = lax.rem(from_z + 2 * pj, NZ) * (NX * ZR) + lax.rem(x + step_x, NX) * ZR + pr
    perm[...] = (lax.broadcasted_iota(jnp.int32, (D, D), 0) == source).astype(jnp.bfloat16)

    def permute(s):
        rows = slice(s * SP, (s + 1) * SP)
        a_perm[rows, :] = jnp.dot(a_all[rows, :], perm[...], preferred_element_type=jnp.float32).astype(jnp.bfloat16)

    permute(0)
    for copy, slot in zip(reversed(a_copies), (1, 3, 2)):
        copy.wait_recv()
        permute(slot)
    whole(g_all.at[:, pl.ds(0, SP)], own_sem)

    def scale_of(level):
        return jnp.exp2(level.astype(jnp.float32) * (1.0 / 64.0))

    def pack(piece):
        half = piece.shape[0] // 2
        top = jnp.maximum(jnp.max(jnp.abs(piece), axis=0, keepdims=True), 1e-30)
        level = jnp.ceil(jnp.log2(top) * 64.0).astype(jnp.int32) + 1
        ints = jnp.round(piece * (LEVELS / scale_of(level))).astype(jnp.int32)
        return ints[:half] * 65536 + ints[half:], level

    def unpack(words, level, weight):
        high = (words + 32768) >> 16
        low = words - high * 65536
        scale = scale_of(level) * (weight * (1.0 / LEVELS))
        return high.astype(jnp.float32) * scale, low.astype(jnp.float32) * scale

    half = D // 2
    p_copies = {}
    for b in range(2):
        for k in range(CH):
            whole(g_all.at[b, pl.ds(SP, 3 * SP), pl.ds(k * CW, CW)], g_recv.at[b, k])
            cols = slice(k * CW, (k + 1) * CW)
            for h in range(2):
                block = lax.dot_general(
                    a_perm[:, h * half:(h + 1) * half], g_all[b, :, cols], (((0,), (0,)), ((), ())),
                    preferred_element_type=jnp.float32)
                if b:
                    half_sum[h * half:(h + 1) * half, cols] = block
                    continue
                words, level = pack(block)
                p_out[k, h, 0:half // 2, :] = words
                p_out[k, h, half // 2:, :] = level
                copy = pltpu.make_async_remote_copy(
                    src_ref=p_out.at[k, h], dst_ref=p_in.at[k, h],
                    send_sem=p_send, recv_sem=p_recv.at[k, h], device_id=at_y(-mate, 0), device_id_type=MESH)
                copy.start()
                p_copies[k, h] = copy
    whole(a_all.at[pl.ds(SP, 3 * SP)], a_send)
    whole(g_all.at[:, pl.ds(SP, 3 * SP)], g_send)

    total = jnp.zeros((1, CW), jnp.float32)
    for k in range(CH):
        cols = slice(k * CW, (k + 1) * CW)
        for h in range(2):
            p_copies[k, h].wait_recv()
            parts_of = unpack(p_in[k, h, 0:half // 2, :], p_in[k, h, half // 2:half // 2 + 1, :], 1.0)
            block = jnp.concatenate(parts_of, axis=0) + half_sum[h * half:(h + 1) * half, cols]
            total = total + jnp.sum(block * block, axis=0, keepdims=True)
            if (k, h) == (CH - 1, 1):
                square = jnp.sum(total, axis=1, keepdims=True)
                row = lax.broadcasted_iota(jnp.int32, (8, 128), 0)
                stat = jnp.where(row < 4, jnp.broadcast_to(square, (8, 128)), jnp.broadcast_to(mask, (8, 128)))
                stat_out[...] = stat
                for i, (dy, dc) in enumerate(aug_peers):
                    copy = pltpu.make_async_remote_copy(
                        src_ref=stat_out, dst_ref=stat_in.at[i], send_sem=s_send, recv_sem=s_recv,
                        device_id=at_y(dy, dc), device_id_type=MESH)
                    copy.start()
            if h == 1:
                own_part[:, cols] = block[3 * XR:]
            for t in range(4 - h):
                words, level = pack(block[t * XR:(t + 1) * XR])
                n = h * 4 + t
                x_out[k, n, 0:XR // 2, :] = words
                x_out[k, n, XR // 2:, :] = level
                copy = pltpu.make_async_remote_copy(
                    src_ref=x_out.at[k, n], dst_ref=x_in.at[k, n],
                    send_sem=x_send, recv_sem=x_recv.at[k], device_id=in_group(*GROUP[n]), device_id_type=MESH)
                copy.start()

    pl.semaphore_wait(met.at[2], 2)

    whole(stat_in, s_recv)
    near = (stat + stat_in[0]) + (stat_in[3] + stat_in[4])
    far = (stat_in[1] + stat_in[2]) + (stat_in[5] + stat_in[6])
    stat = near + far
    count = stat[4:5, :]
    root = jnp.sqrt(stat[0:1, :])
    weight = CLIP / jnp.maximum(root, CLIP * count)
    fac_out[...] = jnp.broadcast_to(weight, (8, 128))
    for n in range(7):
        copy = pltpu.make_async_remote_copy(
            src_ref=fac_out, dst_ref=fac_in.at[n], send_sem=f_send, recv_sem=f_recv,
            device_id=in_group(*GROUP[n]), device_id_type=MESH)
        copy.start()

    norm_ref[...] = (root / count)[:, 0:1]
    half = XR // 2
    for k in range(CH):
        cols = slice(k * CW, (k + 1) * CW)
        whole(x_in.at[k], x_recv.at[k])
        for n in range(7):
            high, low = unpack(x_in[k, n, 0:half, :], x_in[k, n, half:half + 1, :], 1.0)
            x_part[n, 0:half, cols] = high
            x_part[n, half:, cols] = low
    whole(fac_in, f_recv)
    for k in range(CH):
        cols = slice(k * CW, (k + 1) * CW)
        part = weight * own_part[:, cols]
        for n in range(7):
            part = part + fac_in[n, 0:1, :] * x_part[n, :, cols]
        parts[:, cols] = part

    z_copies = []
    for d in Z_ORDER:
        words, level = pack(parts[d * ZR:(d + 1) * ZR, :])
        if d == 0:
            own_ref[0:6, :], own_ref[6:12, :] = unpack(words, level, 1.0)
            continue
        z_out[d - 1, 0:6, :] = words
        z_out[d - 1, 6:7, :] = level
        copy = pltpu.make_async_remote_copy(
            src_ref=z_out.at[d - 1], dst_ref=z_in.at[d - 1], send_sem=z_send, recv_sem=z_recv.at[d - 1],
            device_id=at_z(2 * d), device_id_type=MESH)
        copy.start()
        z_copies.append((d, copy))

    whole(p_out, p_send)
    whole(x_out, x_send)
    whole(stat_in, s_send)
    whole(fac_in, f_send)
    top_rows = low_rows = None
    for d, copy in reversed(z_copies):
        copy.wait_recv()
        words = z_in[d - 1]
        one, two = unpack(words[0:6], words[6:7], 1.0)
        top_rows = one if top_rows is None else top_rows + one
        low_rows = two if low_rows is None else low_rows + two
    rest_ref[0:6, :] = top_rows
    rest_ref[6:12, :] = low_rows

    whole(z_out, z_send)


def per_device(activations, out_grads, kept_mask, noise_field):
    vmem = pl.BlockSpec(memory_space=pltpu.VMEM)
    hbm = pl.BlockSpec(memory_space=pl.ANY)
    dma = pltpu.SemaphoreType.DMA
    bf16, f32, i32 = jnp.bfloat16, jnp.float32, jnp.int32
    own, rest, norm = pl.pallas_call(
        kernel,
        out_shape=(
            jax.ShapeDtypeStruct((ZR, BW), f32), jax.ShapeDtypeStruct((ZR, BW), f32), jax.ShapeDtypeStruct((1, 1), f32)),
        in_specs=[hbm, hbm, vmem],
        out_specs=(vmem,) * 3,
        scratch_shapes=[
            pltpu.VMEM((S, D), bf16),
            pltpu.VMEM((S, FF), bf16),
            pltpu.VMEM((4 * SP, D), bf16),
            pltpu.VMEM((4 * SP, D), bf16),
            pltpu.VMEM((SP, FF), bf16),
            pltpu.VMEM((2, 4 * SP, BW), bf16),
            pltpu.VMEM((D, D), bf16),
            pltpu.VMEM((D, BW), f32),
            pltpu.VMEM((CH, 2, D // 4 + 1, CW), i32),
            pltpu.VMEM((CH, 2, D // 4 + 1, CW), i32),
            pltpu.VMEM((XR, BW), f32),
            pltpu.VMEM((CH, 7, XR // 2 + 1, CW), i32),
            pltpu.VMEM((CH, 7, XR // 2 + 1, CW), i32),
            pltpu.VMEM((7, XR, BW), f32),
            pltpu.VMEM((XR, BW), f32),
            pltpu.VMEM((8, 128), f32),
            pltpu.VMEM((7, 8, 128), f32),
            pltpu.VMEM((8, 128), f32),
            pltpu.VMEM((7, 8, 128), f32),
            pltpu.VMEM((7, 7, BW), i32),
            pltpu.VMEM((7, 7, BW), i32),
            dma((2,)), dma, dma((3,)), dma, dma((2, CH)), dma, dma((CH, 2)), dma, dma((CH,)),
            dma, dma, dma, dma, dma, dma((7,)), dma, pltpu.SemaphoreType.REGULAR((3,)),
        ],
        compiler_params=pltpu.CompilerParams(collective_id=0, has_side_effects=True, vmem_limit_bytes=53 * 2**20 + 700000),
        name="clipped_sum",
    )(activations[0, 0], out_grads[0, 0], kept_mask)
    clipped = own + rest
    update = (clipped + CLIP * noise_field) * (1.0 / IMAGES)
    return clipped, update, norm.reshape(1)


def solution(mesh):
    in_specs = (
        P("img", "aug", None, None),
        P("img", "aug", None, None),
        P("img", "aug"),
        P("img", "aug"),
    )
    out_specs = (P("img", "aug"), P("img", "aug"), P("img"))
    return jax.shard_map(
        per_device, mesh=mesh, in_specs=in_specs, out_specs=out_specs, check_vma=False
    )
```

time: 57.2 us -> 55.7 us (0.974)
  Pallas kernels: 53.3 us -> 51.6 us
    pallas_call x1, Pallas kernels: 53.3 us -> 51.6 us  [per_device(): pl.pallas_call(kernel, out_shape=(jax.ShapeDtypeStruct((ZR, BW), f32), ja...]
where the time goes in v6:
time: 55.7 us; the launch traced here: 55.3 us
  Pallas kernels  51.6 us (93%)
  between operations  3.07 us (6%)
  other arithmetic  0.62 us (1%)
    pallas_call x1, Pallas kernels, per_device(): pl.pallas_call(kernel, out_shape=(jax.ShapeDtypeStruct((ZR, BW), f32), ja...  51.6 us

profile of v6, /device:TPU:1, one launch (start us, length us, event | category | flops | bytes accessed | tf_op | source)
XLA Modules:
  0.0 55.3 jit_solution(11063824817839493557)
XLA Ops:
  0.6 0.0 copy-start
  1.3 51.6 %clipped_sum.1 = (f32[12,384]{1,0:T(8,128)S(1)}, f32[12,384]{1,0:T(8,128)S(1)}, f32[1,1]{1,0:T(1,128)}) custom-call(bf16[197,768]{1,0:T(8,128)(2,1)} %bitcast.4, bf16[197,3072]{1,0:T(8,128)(2,1)} %bitcast.3, s32[1,1]{1,0:T(1,128)S(6)} %copy.8.m_ref), custom_call_target="tpu_custom_call" | custom-call | tf_op jit(solution)/shard_map/clipped_sum/pallas_call | solution.py:277
  52.9 0.0 copy-done
  52.9 0.6 %add_multiply_fusion = (f32[12,384]{1,0:T(8,128)}, f32[12,384]{1,0:T(8,128)}) fusion(f32[12,384]{1,0:T(8,128)S(1)} %copy-done, f32[12,384]{1,0:T(8,128)S(1)} %get-tuple-element.6, f32[12,384]{1,0:T(8,128)S(1)} %get-tuple-element.7), kind=kLoop, calls=%fused_computation | loop fusion | flops 18432 | bytes 92160 | tf_op jit(solution)/shard_map/mul | solution.py:312
Async XLA Ops:
  0.6 52.3 %copy-start = (f32[12,384]{1,0:T(8,128)S(1)}, f32[12,384]{1,0:T(8,128)}, u32[]{:S(2)}) copy-start(f32[12,384]{1,0:T(8,128)} %param.7) | copy-start | bytes 55300

commit v7 on v6

--- a/solution.py
+++ b/solution.py
@@ -12,6 +12,7 @@
 NZ, NX, NY = 16, 4, 4
 S, D, FF = 197, 768, 3072
 SP = 208
+MAIN = 192
 BW = FF // 8
 CH = 3
 CW = BW // CH
@@ -25,11 +26,11 @@
 
 
 def kernel(
-    a_hbm, g_hbm, m_ref,
-    own_ref, rest_ref, norm_ref,
-    a_raw, g_raw, a_all, a_perm, g_pad, g_all, perm, half_sum, p_out, p_in, own_part, x_out, x_in, x_part, parts,
+    a_hbm, g_hbm, m_hbm,
+    own_ref, rest_ref,
+    a_raw, g_raw, m_ref, tail32, tail_out, tail_in, a_all, a_perm, g_all, perm, half_sum, p_out, p_in, own_part, x_out, x_in, x_part, parts,
     stat_out, stat_in, fac_out, fac_in, z_out, z_in,
-    in_sem, a_send, a_recv, g_send, g_recv, p_send, p_recv, x_send, x_recv, s_send, s_recv, f_send, f_recv, z_send, z_recv, own_sem, met,
+    in_sem, t_send, t_recv, a_send, a_recv, g_send, g_recv, p_send, p_recv, x_send, x_recv, s_send, s_recv, f_send, f_recv, z_send, z_recv, met,
 ):
     img, aug = lax.axis_index("img"), lax.axis_index("aug")
     z, x, y, c = img // NX, lax.rem(img, NX), aug // 2, lax.rem(aug, 2)
@@ -65,14 +66,20 @@
 
     a_load = pltpu.make_async_copy(a_hbm, a_raw, in_sem.at[0])
     g_load = pltpu.make_async_copy(g_hbm, g_raw, in_sem.at[1])
+    m_load = pltpu.make_async_copy(m_hbm, m_ref, in_sem.at[2])
+    m_load.start()
     a_load.start()
     g_load.start()
 
-    mask = m_ref[...].astype(jnp.float32)
-    a_load.wait()
-    a_all[0:192, :] = (a_raw[0:192, :].astype(jnp.float32) * mask).astype(jnp.bfloat16)
-    a_all[192:SP, :] = jnp.zeros((SP - 192, D), jnp.bfloat16)
-    a_all[192:S, :] = (a_raw[192:S, :].astype(jnp.float32) * mask).astype(jnp.bfloat16)
+    def columns(block, k, width):
+        return pl.ds(pl.multiple_of(block * BW + k * CW, CW), width)
+
+    own_copies = [pltpu.make_async_copy(a_hbm.at[pl.ds(0, MAIN)], a_all.at[0, pl.ds(0, MAIN)], in_sem.at[3])]
+    for b, block in enumerate((block_of(-mate, 0), block_of(0, 0))):
+        own_copies.append(pltpu.make_async_copy(
+            g_hbm.at[pl.ds(0, MAIN), columns(block, 0, BW)], g_all.at[b, 0, pl.ds(0, MAIN)], in_sem.at[4 + b]))
+    for copy in own_copies:
+        copy.start()
 
     pl.semaphore_wait(barrier, 9)
 
@@ -88,33 +95,43 @@
     a_copies = []
     for slot, device, _ in partners:
         copy = pltpu.make_async_remote_copy(
-            src_ref=a_all.at[pl.ds(0, SP)], dst_ref=a_all.at[pl.ds(slot * SP, SP)],
+            src_ref=a_hbm.at[pl.ds(0, MAIN)], dst_ref=a_all.at[slot, pl.ds(0, MAIN)],
             send_sem=a_send, recv_sem=a_recv.at[slot - 1], device_id=at_y(*device), device_id_type=MESH)
         copy.start()
         a_copies.append(copy)
 
-    pl.semaphore_wait(met.at[0], 5)
-    call(1, [in_group(1, 0), at_z(2), at_z(-2)])
+    m_load.wait()
+    mask = m_ref[...].astype(jnp.float32)
+    a_load.wait()
     g_load.wait()
-    g_pad[0:192, :] = g_raw[0:192, :]
-    g_pad[192:SP, :] = jnp.zeros((SP - 192, FF), jnp.bfloat16)
-    g_pad[192:S, :] = g_raw[192:S, :]
-    def columns(block, k, width):
-        return pl.ds(pl.multiple_of(block * BW + k * CW, CW), width)
-
-    for b, block in enumerate((block_of(-mate, 0), block_of(0, 0))):
-        copy = pltpu.make_async_copy(g_pad.at[:, columns(block, 0, BW)], g_all.at[b, pl.ds(0, SP)], own_sem)
-        copy.start()
+    tail32[...] = jnp.zeros_like(tail32)
+    targets = [(0, (), ((-mate, 0), (0, 0)))] + list(partners)
+    for i, (slot, device, blocks) in enumerate(targets):
+        tail32[i, 0:S - MAIN, :] = a_raw[MAIN:S, :].astype(jnp.float32)
+        tail32[i, 5:6, :] = jnp.broadcast_to(mask, (1, D))
+        for b in range(2):
+            tail32[i, 8:8 + S - MAIN, b * BW:(b + 1) * BW] = g_raw[
+                MAIN:S, columns(block_of(*blocks[b]), 0, BW)].astype(jnp.float32)
+        if slot == 0:
+            tail_in[0] = tail32[i].astype(jnp.bfloat16)
+            continue
+        tail_out[i - 1] = tail32[i].astype(jnp.bfloat16)
+        pltpu.make_async_remote_copy(
+            src_ref=tail_out.at[i - 1], dst_ref=tail_in.at[slot], send_sem=t_send, recv_sem=t_recv,
+            device_id=at_y(*device), device_id_type=MESH).start()
+
     for b in range(2):
         for k in range(CH):
             for slot, device, blocks in partners:
                 copy = pltpu.make_async_remote_copy(
-                    src_ref=g_pad.at[:, columns(block_of(*blocks[b]), k, CW)],
-                    dst_ref=g_all.at[b, pl.ds(slot * SP, SP), pl.ds(k * CW, CW)],
+                    src_ref=g_raw.at[pl.ds(0, MAIN), columns(block_of(*blocks[b]), k, CW)],
+                    dst_ref=g_all.at[b, slot, pl.ds(0, MAIN), pl.ds(k * CW, CW)],
                     send_sem=g_send, recv_sem=g_recv.at[b, k],
                     device_id=at_y(*device), device_id_type=MESH)
                 copy.start()
 
+    pl.semaphore_wait(met.at[0], 5)
+    call(1, [in_group(1, 0), at_z(2), at_z(-2)])
     pl.semaphore_wait(met.at[1], 3)
     call(2, [at_z(4), at_z(-4)])
 
@@ -126,14 +143,23 @@
     perm[...] = (lax.broadcasted_iota(jnp.int32, (D, D), 0) == source).astype(jnp.bfloat16)
 
     def permute(s):
-        rows = slice(s * SP, (s + 1) * SP)
-        a_perm[rows, :] = jnp.dot(a_all[rows, :], perm[...], preferred_element_type=jnp.float32).astype(jnp.bfloat16)
-
+        tail = tail_in[s].astype(jnp.float32)
+        row = lax.broadcasted_iota(jnp.int32, (16, D), 0)
+        a_all[s, MAIN:SP, :] = jnp.where(row < S - MAIN, tail, 0.0).astype(jnp.bfloat16)
+        grads = jnp.where(row[0:8] < S - MAIN, tail[8:16], 0.0)
+        grads = jnp.concatenate([grads, jnp.zeros((8, D), jnp.float32)], axis=0).astype(jnp.bfloat16)
+        for b in range(2):
+            g_all[b, s, MAIN:SP, :] = grads[:, b * BW:(b + 1) * BW]
+        product = jnp.dot(a_all[s], perm[...], preferred_element_type=jnp.float32)
+        a_perm[s * SP:(s + 1) * SP, :] = (product * tail[5:6, :]).astype(jnp.bfloat16)
+
+    for copy in own_copies:
+        copy.wait()
     permute(0)
+    whole(tail_in.at[pl.ds(1, 3)], t_recv)
     for copy, slot in zip(reversed(a_copies), (1, 3, 2)):
         copy.wait_recv()
         permute(slot)
-    whole(g_all.at[:, pl.ds(0, SP)], own_sem)
 
     def scale_of(level):
         return jnp.exp2(level.astype(jnp.float32) * (1.0 / 64.0))
@@ -155,11 +181,11 @@
     p_copies = {}
     for b in range(2):
         for k in range(CH):
-            whole(g_all.at[b, pl.ds(SP, 3 * SP), pl.ds(k * CW, CW)], g_recv.at[b, k])
+            whole(g_all.at[b, pl.ds(1, 3), pl.ds(0, MAIN), pl.ds(k * CW, CW)], g_recv.at[b, k])
             cols = slice(k * CW, (k + 1) * CW)
             for h in range(2):
                 block = lax.dot_general(
-                    a_perm[:, h * half:(h + 1) * half], g_all[b, :, cols], (((0,), (0,)), ((), ())),
+                    a_perm[:, h * half:(h + 1) * half], g_all[b, :, :, cols].reshape(4 * SP, CW), (((0,), (0,)), ((), ())),
                     preferred_element_type=jnp.float32)
                 if b:
                     half_sum[h * half:(h + 1) * half, cols] = block
@@ -172,8 +198,9 @@
                     send_sem=p_send, recv_sem=p_recv.at[k, h], device_id=at_y(-mate, 0), device_id_type=MESH)
                 copy.start()
                 p_copies[k, h] = copy
-    whole(a_all.at[pl.ds(SP, 3 * SP)], a_send)
-    whole(g_all.at[:, pl.ds(SP, 3 * SP)], g_send)
+    whole(a_all.at[pl.ds(1, 3), pl.ds(0, MAIN)], a_send)
+    whole(g_all.at[:, pl.ds(1, 3), pl.ds(0, MAIN)], g_send)
+    whole(tail_out, t_send)
 
     total = jnp.zeros((1, CW), jnp.float32)
     for k in range(CH):
@@ -221,7 +248,7 @@
             device_id=in_group(*GROUP[n]), device_id_type=MESH)
         copy.start()
 
-    norm_ref[...] = (root / count)[:, 0:1]
+    rest_ref[ZR:ZR + 1, 0:128] = root / count
     half = XR // 2
     for k in range(CH):
         cols = slice(k * CW, (k + 1) * CW)
@@ -274,19 +301,21 @@
     hbm = pl.BlockSpec(memory_space=pl.ANY)
     dma = pltpu.SemaphoreType.DMA
     bf16, f32, i32 = jnp.bfloat16, jnp.float32, jnp.int32
-    own, rest, norm = pl.pallas_call(
+    own, rest = pl.pallas_call(
         kernel,
-        out_shape=(
-            jax.ShapeDtypeStruct((ZR, BW), f32), jax.ShapeDtypeStruct((ZR, BW), f32), jax.ShapeDtypeStruct((1, 1), f32)),
-        in_specs=[hbm, hbm, vmem],
-        out_specs=(vmem,) * 3,
+        out_shape=(jax.ShapeDtypeStruct((ZR, BW), f32), jax.ShapeDtypeStruct((16, BW), f32)),
+        in_specs=[hbm, hbm, hbm],
+        out_specs=(vmem,) * 2,
         scratch_shapes=[
             pltpu.VMEM((S, D), bf16),
             pltpu.VMEM((S, FF), bf16),
+            pltpu.VMEM((1, 1), i32),
+            pltpu.VMEM((4, 16, D), f32),
+            pltpu.VMEM((3, 16, D), bf16),
+            pltpu.VMEM((4, 16, D), bf16),
+            pltpu.VMEM((4, SP, D), bf16),
             pltpu.VMEM((4 * SP, D), bf16),
-            pltpu.VMEM((4 * SP, D), bf16),
-            pltpu.VMEM((SP, FF), bf16),
-            pltpu.VMEM((2, 4 * SP, BW), bf16),
+            pltpu.VMEM((2, 4, SP, BW), bf16),
             pltpu.VMEM((D, D), bf16),
             pltpu.VMEM((D, BW), f32),
             pltpu.VMEM((CH, 2, D // 4 + 1, CW), i32),
@@ -302,15 +331,15 @@
             pltpu.VMEM((7, 8, 128), f32),
             pltpu.VMEM((7, 7, BW), i32),
             pltpu.VMEM((7, 7, BW), i32),
-            dma((2,)), dma, dma((3,)), dma, dma((2, CH)), dma, dma((CH, 2)), dma, dma((CH,)),
-            dma, dma, dma, dma, dma, dma((7,)), dma, pltpu.SemaphoreType.REGULAR((3,)),
+            dma((6,)), dma, dma, dma, dma((3,)), dma, dma((2, CH)), dma, dma((CH, 2)), dma, dma((CH,)),
+            dma, dma, dma, dma, dma, dma((7,)), pltpu.SemaphoreType.REGULAR((3,)),
         ],
         compiler_params=pltpu.CompilerParams(collective_id=0, has_side_effects=True, vmem_limit_bytes=53 * 2**20 + 700000),
         name="clipped_sum",
     )(activations[0, 0], out_grads[0, 0], kept_mask)
-    clipped = own + rest
+    clipped = own + rest[:ZR]
     update = (clipped + CLIP * noise_field) * (1.0 / IMAGES)
-    return clipped, update, norm.reshape(1)
+    return clipped, update, rest[ZR, :1]
 
 
 def solution(mesh):

time: 55.7 us -> 53.6 us (0.962)
  between operations: 3.07 us -> 1.31 us
  Pallas kernels: 51.6 us -> 50.7 us
    pallas_call x1, Pallas kernels: 51.6 us -> 50.7 us  [per_device(): pl.pallas_call(kernel, out_shape=(jax.ShapeDtypeStruct((ZR, BW), f32), ja...]
where the time goes in v7:
time: 53.6 us; the launch traced here: 53.2 us
  Pallas kernels  50.7 us (95%)
  between operations  1.31 us (2%)
  other arithmetic  0.62 us (1%)
    pallas_call x1, Pallas kernels, per_device(): pl.pallas_call(kernel, out_shape=(jax.ShapeDtypeStruct((ZR, BW), f32), ja...  50.7 us

profile of v7, /device:TPU:1, one launch (start us, length us, event | category | flops | bytes accessed | tf_op | source)
XLA Modules:
  0.0 53.2 jit_solution(4660780157359534512)
XLA Ops:
  0.6 0.0 copy-start
  1.3 50.7 %clipped_sum.1 = (f32[12,384]{1,0:T(8,128)S(1)}, f32[16,384]{1,0:T(8,128)S(1)}) custom-call(bf16[197,768]{1,0:T(8,128)(2,1)} %bitcast.4, bf16[197,3072]{1,0:T(8,128)(2,1)} %bitcast.3, s32[1,1]{1,0:T(1,128)S(6)} %copy.7.m_hbm), custom_call_target="tpu_custom_call" | custom-call | tf_op jit(solution)/shard_map/clipped_sum/pallas_call | solution.py:304
  52.0 0.0 copy-done
  52.1 0.6 %add_multiply_fusion = (f32[12,384]{1,0:T(8,128)}, f32[12,384]{1,0:T(8,128)}) fusion(f32[12,384]{1,0:T(8,128)S(1)} %copy-done, f32[12,384]{1,0:T(8,128)S(1)} %get-tuple-element.5, f32[16,384]{1,0:T(8,128)S(1)} %get-tuple-element.6), kind=kLoop, calls=%fused_computation | loop fusion | flops 18432 | bytes 92160 | tf_op jit(solution)/shard_map/mul | solution.py:341
  52.7 0.5 slice.7
Async XLA Ops:
  0.6 51.4 %copy-start = (f32[12,384]{1,0:T(8,128)S(1)}, f32[12,384]{1,0:T(8,128)}, u32[]{:S(2)}) copy-start(f32[12,384]{1,0:T(8,128)} %param.7) | copy-start | bytes 55300

commit v8 on v7

--- a/solution.py
+++ b/solution.py
@@ -22,7 +22,7 @@
 CLIP = 0.01 * math.sqrt(D * FF * S)
 LEVELS = 32766.0
 GROUP = ((2, 1), (2, 0), (1, 1), (1, 0), (3, 1), (3, 0), (0, 1), (0, 0))
-Z_ORDER = (4, 3, 5, 2, 6, 1, 7, 0)
+Z_ORDER = (7, 6, 5, 4, 3, 2, 1, 0)
 
 
 def kernel(
@@ -44,6 +44,9 @@
         return lax.rem(y + dy + NY, NY) * 2 + lax.rem(c + dc, 2)
 
     pair = z + 1 - 2 * lax.rem(z, 2)
+
+    def z_step(of):
+        return 1 - 2 * lax.rem(of + 1, 2)
 
     def in_group(dx, other):
         return ((pair if other else z) * NX + lax.rem(x + dx, NX), aug)
@@ -139,7 +142,7 @@
     pn, pj, pr = p // XR, lax.rem(p, XR) // ZR, lax.rem(p, ZR)
     step_x = jnp.where(pn < 2, 2, jnp.where(pn < 4, 1, jnp.where(pn < 6, 3, 0)))
     from_z = jnp.where(lax.rem(pn, 2) == 0, pair, z)
-    source = lax.rem(from_z + 2 * pj, NZ) * (NX * ZR) + lax.rem(x + step_x, NX) * ZR + pr
+    source = lax.rem(from_z + z_step(from_z) * pj + NZ, NZ) * (NX * ZR) + lax.rem(x + step_x, NX) * ZR + pr
     perm[...] = (lax.broadcasted_iota(jnp.int32, (D, D), 0) == source).astype(jnp.bfloat16)
 
     def permute(s):
@@ -275,7 +278,7 @@
         z_out[d - 1, 6:7, :] = level
         copy = pltpu.make_async_remote_copy(
             src_ref=z_out.at[d - 1], dst_ref=z_in.at[d - 1], send_sem=z_send, recv_sem=z_recv.at[d - 1],
-            device_id=at_z(2 * d), device_id_type=MESH)
+            device_id=at_z(z_step(z) * d), device_id_type=MESH)
         copy.start()
         z_copies.append((d, copy))
 
@@ -294,6 +297,13 @@
     rest_ref[6:12, :] = low_rows
 
     whole(z_out, z_send)
+
+
+def finish(own_ref, rest_ref, noise_ref, clip_ref, upd_ref, norm_ref):
+    clipped = own_ref[...] + rest_ref[0:ZR, :]
+    clip_ref[...] = clipped
+    upd_ref[...] = (clipped + CLIP * noise_ref[...]) * (1.0 / IMAGES)
+    norm_ref[0] = jnp.max(rest_ref[ZR:ZR + 1, 0:128])
 
 
 def per_device(activations, out_grads, kept_mask, noise_field):
@@ -337,9 +347,16 @@
         compiler_params=pltpu.CompilerParams(collective_id=0, has_side_effects=True, vmem_limit_bytes=53 * 2**20 + 700000),
         name="clipped_sum",
     )(activations[0, 0], out_grads[0, 0], kept_mask)
-    clipped = own + rest[:ZR]
-    update = (clipped + CLIP * noise_field) * (1.0 / IMAGES)
-    return clipped, update, rest[ZR, :1]
+    clipped, update, norm = pl.pallas_call(
+        finish,
+        out_shape=(
+            jax.ShapeDtypeStruct((ZR, BW), f32), jax.ShapeDtypeStruct((ZR, BW), f32), jax.ShapeDtypeStruct((1,), f32)),
+        in_specs=[vmem] * 3,
+        out_specs=(vmem, vmem, pl.BlockSpec(memory_space=pltpu.SMEM)),
+        compiler_params=pltpu.CompilerParams(vmem_limit_bytes=2**20),
+        name="update",
+    )(own, rest, noise_field)
+    return clipped, update, norm
 
 
 def solution(mesh):

time: 53.6 us -> 52.5 us (0.979)
  other arithmetic: 0.62 us -> 0 us
    pallas_call x0 -> x1, Pallas kernels: none -> 0.63 us  [per_device(): pl.pallas_call(finish, out_shape=(jax.ShapeDtypeStruct((ZR, BW), f32), ja...]
    mul x1 -> x0, other arithmetic: 0.62 us -> none  [per_device(): update = (clipped + CLIP * noise_field) * (1.0 / IMAGES)]
where the time goes in v8:
time: 52.5 us; the launch traced here: 52.4 us
  Pallas kernels  51 us (97%)
  between operations  1.31 us (2%)
    pallas_call x1, Pallas kernels, per_device(): pl.pallas_call(kernel, out_shape=(jax.ShapeDtypeStruct((ZR, BW), f32), ja...  50.4 us

profile of v8, /device:TPU:1, one launch (start us, length us, event | category | flops | bytes accessed | tf_op | source)
XLA Modules:
  0.0 52.4 jit_solution(5915102060981877841)
XLA Ops:
  0.6 0.0 copy-start
  1.3 50.4 %clipped_sum.1 = (f32[12,384]{1,0:T(8,128)S(1)}, f32[16,384]{1,0:T(8,128)S(1)}) custom-call(bf16[197,768]{1,0:T(8,128)(2,1)} %bitcast.3, bf16[197,3072]{1,0:T(8,128)(2,1)} %bitcast.2, s32[1,1]{1,0:T(1,128)S(6)} %copy.7.m_hbm), custom_call_target="tpu_custom_call" | custom-call | tf_op jit(solution)/shard_map/clipped_sum/pallas_call | solution.py:314
  51.7 0.0 copy-done
  51.7 0.6 %update.1 = (f32[12,384]{1,0:T(8,128)}, f32[12,384]{1,0:T(8,128)}, f32[1]{0:T(128)}) custom-call(f32[12,384]{1,0:T(8,128)S(1)} %get-tuple-element.5.own_ref, f32[16,384]{1,0:T(8,128)S(1)} %get-tuple-element.6.rest_ref, f32[12,384]{1,0:T(8,128)S(1)} %copy-done), custom_call_target="tpu_custom_call" | custom-call | tf_op jit(solution)/shard_map/update/pallas_call | solution.py:350
Async XLA Ops:
  0.6 51.1 %copy-start = (f32[12,384]{1,0:T(8,128)S(1)}, f32[12,384]{1,0:T(8,128)}, u32[]{:S(2)}) copy-start(f32[12,384]{1,0:T(8,128)} %noise_ref.1) | copy-start | bytes 55300

commit v9 on v8

--- a/solution.py
+++ b/solution.py
@@ -67,30 +67,11 @@
     for device in next_to:
         pl.semaphore_signal(barrier, inc=1, device_id=device, device_id_type=MESH)
 
-    a_load = pltpu.make_async_copy(a_hbm, a_raw, in_sem.at[0])
-    g_load = pltpu.make_async_copy(g_hbm, g_raw, in_sem.at[1])
-    m_load = pltpu.make_async_copy(m_hbm, m_ref, in_sem.at[2])
-    m_load.start()
-    a_load.start()
-    g_load.start()
-
-    def columns(block, k, width):
-        return pl.ds(pl.multiple_of(block * BW + k * CW, CW), width)
-
-    own_copies = [pltpu.make_async_copy(a_hbm.at[pl.ds(0, MAIN)], a_all.at[0, pl.ds(0, MAIN)], in_sem.at[3])]
-    for b, block in enumerate((block_of(-mate, 0), block_of(0, 0))):
-        own_copies.append(pltpu.make_async_copy(
-            g_hbm.at[pl.ds(0, MAIN), columns(block, 0, BW)], g_all.at[b, 0, pl.ds(0, MAIN)], in_sem.at[4 + b]))
-    for copy in own_copies:
-        copy.start()
-
     pl.semaphore_wait(barrier, 9)
 
     def call(step, devices):
         for device in devices:
             pl.semaphore_signal(met.at[step], inc=1, device_id=device, device_id_type=MESH)
-
-    call(0, [at_y(1, 0), in_group(1, 0), in_group(NX - 1, 0), at_z(1), at_z(-1)])
 
     def whole(ref, sem):
         pltpu.make_async_copy(ref, ref, sem).wait()
@@ -102,6 +83,25 @@
             send_sem=a_send, recv_sem=a_recv.at[slot - 1], device_id=at_y(*device), device_id_type=MESH)
         copy.start()
         a_copies.append(copy)
+
+    call(0, [at_y(1, 0), in_group(1, 0), in_group(NX - 1, 0), at_z(1), at_z(-1)])
+
+    a_load = pltpu.make_async_copy(a_hbm, a_raw, in_sem.at[0])
+    g_load = pltpu.make_async_copy(g_hbm, g_raw, in_sem.at[1])
+    m_load = pltpu.make_async_copy(m_hbm, m_ref, in_sem.at[2])
+    m_load.start()
+    a_load.start()
+    g_load.start()
+
+    def columns(block, k, width):
+        return pl.ds(pl.multiple_of(block * BW + k * CW, CW), width)
+
+    own_copies = [pltpu.make_async_copy(a_hbm.at[pl.ds(0, MAIN)], a_all.at[0, pl.ds(0, MAIN)], in_sem.at[3])]
+    for b, block in enumerate((block_of(-mate, 0), block_of(0, 0))):
+        own_copies.append(pltpu.make_async_copy(
+            g_hbm.at[pl.ds(0, MAIN), columns(block, 0, BW)], g_all.at[b, 0, pl.ds(0, MAIN)], in_sem.at[4 + b]))
+    for copy in own_copies:
+        copy.start()
 
     m_load.wait()
     mask = m_ref[...].astype(jnp.float32)
@@ -211,14 +211,17 @@
         for h in range(2):
             p_copies[k, h].wait_recv()
             parts_of = unpack(p_in[k, h, 0:half // 2, :], p_in[k, h, half // 2:half // 2 + 1, :], 1.0)
-            block = jnp.concatenate(parts_of, axis=0) + half_sum[h * half:(h + 1) * half, cols]
-            total = total + jnp.sum(block * block, axis=0, keepdims=True)
+            high = parts_of[0] + half_sum[h * half:h * half + half // 2, cols]
+            low = parts_of[1] + half_sum[h * half + half // 2:(h + 1) * half, cols]
+            total = total + jnp.sum(high * high + low * low, axis=0, keepdims=True)
+            block = jnp.concatenate([high, low], axis=0)
             if (k, h) == (CH - 1, 1):
                 square = jnp.sum(total, axis=1, keepdims=True)
                 row = lax.broadcasted_iota(jnp.int32, (8, 128), 0)
                 stat = jnp.where(row < 4, jnp.broadcast_to(square, (8, 128)), jnp.broadcast_to(mask, (8, 128)))
                 stat_out[...] = stat
-                for i, (dy, dc) in enumerate(aug_peers):
+                for i in (3, 4, 1, 2, 5, 6, 0):
+                    dy, dc = aug_peers[i]
                     copy = pltpu.make_async_remote_copy(
                         src_ref=stat_out, dst_ref=stat_in.at[i], send_sem=s_send, recv_sem=s_recv,
                         device_id=at_y(dy, dc), device_id_type=MESH)

time: 52.5 us -> 52.6 us (level)
  no operation moved by 1% of the time
where the time goes in v9:
time: 52.6 us; the launch traced here: 52.4 us
  Pallas kernels  51 us (97%)
  between operations  1.31 us (2%)
    pallas_call x1, Pallas kernels, per_device(): pl.pallas_call(kernel, out_shape=(jax.ShapeDtypeStruct((ZR, BW), f32), ja...  50.4 us

profile of v9, /device:TPU:1, one launch (start us, length us, event | category | flops | bytes accessed | tf_op | source)
XLA Modules:
  0.0 52.4 jit_solution(13885614219646241565)
XLA Ops:
  0.6 0.0 copy-start
  1.3 50.4 %clipped_sum.1 = (f32[12,384]{1,0:T(8,128)S(1)}, f32[16,384]{1,0:T(8,128)S(1)}) custom-call(bf16[197,768]{1,0:T(8,128)(2,1)} %bitcast.3, bf16[197,3072]{1,0:T(8,128)(2,1)} %bitcast.2, s32[1,1]{1,0:T(1,128)S(6)} %copy.7.m_hbm), custom_call_target="tpu_custom_call" | custom-call | tf_op jit(solution)/shard_map/clipped_sum/pallas_call | solution.py:317
  51.7 0.0 copy-done
  51.7 0.6 %update.1 = (f32[12,384]{1,0:T(8,128)}, f32[12,384]{1,0:T(8,128)}, f32[1]{0:T(128)}) custom-call(f32[12,384]{1,0:T(8,128)S(1)} %get-tuple-element.5.own_ref, f32[16,384]{1,0:T(8,128)S(1)} %get-tuple-element.6.rest_ref, f32[12,384]{1,0:T(8,128)S(1)} %copy-done), custom_call_target="tpu_custom_call" | custom-call | tf_op jit(solution)/shard_map/update/pallas_call | solution.py:353
Async XLA Ops:
  0.6 51.1 %copy-start = (f32[12,384]{1,0:T(8,128)S(1)}, f32[12,384]{1,0:T(8,128)}, u32[]{:S(2)}) copy-start(f32[12,384]{1,0:T(8,128)} %noise_ref.1) | copy-start | bytes 55300

commit v10 on v9

--- a/solution.py
+++ b/solution.py
@@ -124,12 +124,13 @@
             device_id=at_y(*device), device_id_type=MESH).start()
 
     for b in range(2):
-        for k in range(CH):
+        for k in range(CH if b == 0 else 1):
+            width = CW if b == 0 else BW
             for slot, device, blocks in partners:
                 copy = pltpu.make_async_remote_copy(
-                    src_ref=g_raw.at[pl.ds(0, MAIN), columns(block_of(*blocks[b]), k, CW)],
-                    dst_ref=g_all.at[b, slot, pl.ds(0, MAIN), pl.ds(k * CW, CW)],
-                    send_sem=g_send, recv_sem=g_recv.at[b, k],
+                    src_ref=g_raw.at[pl.ds(0, MAIN), columns(block_of(*blocks[b]), k, width)],
+                    dst_ref=g_all.at[b, slot, pl.ds(0, MAIN), pl.ds(k * CW, width)],
+                    send_sem=g_send, recv_sem=g_recv.at[k if b == 0 else CH],
                     device_id=at_y(*device), device_id_type=MESH)
                 copy.start()
 
@@ -184,7 +185,10 @@
     p_copies = {}
     for b in range(2):
         for k in range(CH):
-            whole(g_all.at[b, pl.ds(1, 3), pl.ds(0, MAIN), pl.ds(k * CW, CW)], g_recv.at[b, k])
+            if b == 0:
+                whole(g_all.at[0, pl.ds(1, 3), pl.ds(0, MAIN), pl.ds(k * CW, CW)], g_recv.at[k])
+            elif k == 0:
+                whole(g_all.at[1, pl.ds(1, 3), pl.ds(0, MAIN)], g_recv.at[CH])
             cols = slice(k * CW, (k + 1) * CW)
             for h in range(2):
                 block = lax.dot_general(
@@ -344,7 +348,7 @@
             pltpu.VMEM((7, 8, 128), f32),
             pltpu.VMEM((7, 7, BW), i32),
             pltpu.VMEM((7, 7, BW), i32),
-            dma((6,)), dma, dma, dma, dma((3,)), dma, dma((2, CH)), dma, dma((CH, 2)), dma, dma((CH,)),
+            dma((6,)), dma, dma, dma, dma((3,)), dma, dma((CH + 1,)), dma, dma((CH, 2)), dma, dma((CH,)),
             dma, dma, dma, dma, dma, dma((7,)), pltpu.SemaphoreType.REGULAR((3,)),
         ],
         compiler_params=pltpu.CompilerParams(collective_id=0, has_side_effects=True, vmem_limit_bytes=53 * 2**20 + 700000),

time: 52.6 us -> 52.5 us (level)
  no operation moved by 1% of the time
where the time goes in v10:
time: 52.5 us; the launch traced here: 52.3 us
  Pallas kernels  51 us (97%)
  between operations  1.31 us (2%)
    pallas_call x1, Pallas kernels, per_device(): pl.pallas_call(kernel, out_shape=(jax.ShapeDtypeStruct((ZR, BW), f32), ja...  50.4 us

profile of v10, /device:TPU:1, one launch (start us, length us, event | category | flops | bytes accessed | tf_op | source)
XLA Modules:
  0.0 52.3 jit_solution(7828661219061833846)
XLA Ops:
  0.6 0.0 copy-start
  1.3 50.4 %clipped_sum.1 = (f32[12,384]{1,0:T(8,128)S(1)}, f32[16,384]{1,0:T(8,128)S(1)}) custom-call(bf16[197,768]{1,0:T(8,128)(2,1)} %bitcast.3, bf16[197,3072]{1,0:T(8,128)(2,1)} %bitcast.2, s32[1,1]{1,0:T(1,128)S(6)} %copy.7.m_hbm), custom_call_target="tpu_custom_call" | custom-call | tf_op jit(solution)/shard_map/clipped_sum/pallas_call | solution.py:321
  51.7 0.0 copy-done
  51.7 0.6 %update.1 = (f32[12,384]{1,0:T(8,128)}, f32[12,384]{1,0:T(8,128)}, f32[1]{0:T(128)}) custom-call(f32[12,384]{1,0:T(8,128)S(1)} %get-tuple-element.5.own_ref, f32[16,384]{1,0:T(8,128)S(1)} %get-tuple-element.6.rest_ref, f32[12,384]{1,0:T(8,128)S(1)} %copy-done), custom_call_target="tpu_custom_call" | custom-call | tf_op jit(solution)/shard_map/update/pallas_call | solution.py:357
Async XLA Ops:
  0.6 51.1 %copy-start = (f32[12,384]{1,0:T(8,128)S(1)}, f32[12,384]{1,0:T(8,128)}, u32[]{:S(2)}) copy-start(f32[12,384]{1,0:T(8,128)} %noise_ref.1) | copy-start | bytes 55300
